TPU v7x, 32 devices: a whole 2x2x4 slice. The times are simulated.
32 devices in a mesh: shard: 8 (over y, x, core), rep: 4 (over z).
Axes of the slice: x: 2, y: 2, z: 4, core: 2. Of those that a mesh axis runs over, the one named last changes fastest.
Arguments:
- big_images: bfloat16 [32, 32, 32, 384], P(('shard', 'rep')), may hold values from -6 to 6
- small_images: bfloat16 [32, 16, 16, 384], P(('shard', 'rep')), may hold values from -6 to 6
- big_labels: int32 [32], P(('shard', 'rep')), may hold values from 0 to 999
- small_labels: int32 [32], P(('shard', 'rep')), may hold values from 0 to 999
- big_sigmas: int32 [32], P(('shard', 'rep')), may hold values from 0 to 255
- small_sigmas: int32 [32], P(('shard', 'rep')), may hold values from 0 to 255
- loads: int32 [32, 2], P(('shard', 'rep')), may hold values from 0 to 1, as said below
- class_table: bfloat16 [1000, 768], replicated, may hold values from -6 to 6
- sigma_table: bfloat16 [256, 768], replicated, may hold values from -6 to 6
- norm_gains: bfloat16 [3, 384], P(None, 'shard'), may hold values from 0.099609375 to 1.8984375
- biases: bfloat16 [10, 384], P(None, 'shard'), may hold values from -1.796875 to 1.796875
- w_conv0: bfloat16 [3456, 384], P('shard'), may hold values from -0.109375 to 0.109375
- w_conv1: bfloat16 [3456, 384], P('shard'), may hold values from -0.109375 to 0.109375
- w_affine: bfloat16 [768, 768], P('shard'), may hold values from -0.21875 to 0.21875
- w_qkv: bfloat16 [384, 1152], P('shard'), may hold values from -0.3125 to 0.3125
- w_proj: bfloat16 [384, 384], P('shard'), may hold values from -1.25 to 1.25
- big_cotangent: bfloat16 [32, 32, 32, 384], P(('shard', 'rep')), may hold values from -6 to 6
- small_cotangent: bfloat16 [32, 16, 16, 384], P(('shard', 'rep')), may hold values from -6 to 6
Outputs:
- big_output: bfloat16 [32, 32, 32, 384], P(('shard', 'rep'))
- small_output: bfloat16 [32, 16, 16, 384], P(('shard', 'rep'))
- big_grad: bfloat16 [32, 32, 32, 384], P(('shard', 'rep'))
- small_grad: bfloat16 [32, 16, 16, 384], P(('shard', 'rep'))
- grad_norm_gains: float32 [3, 384], P(None, 'shard')
- grad_biases: float32 [10, 384], P(None, 'shard')
- grad_conv0: float32 [3456, 384], P('shard')
- grad_conv1: float32 [3456, 384], P('shard')
- grad_affine: float32 [768, 768], P('shard')
- grad_qkv: float32 [384, 1152], P('shard')
- grad_proj: float32 [384, 384], P('shard')
Inputs may be any that keep to these rules, and one draw needn't show every extreme that they name: Row d of loads belongs to the device holding slots d * 1 onward of the large and d * 1 onward of the small images; column 0 counts its live large images (0 to 1), column 1 its live small images (1 to 1); the live images are the first slots of the device; in every draw some device has all its slots live.
All inputs are finite; a program needn't handle non-finite values.
Results may differ from a plain program's by a relative error of at most 0.017.
Values may be sent and summed in bfloat16 or wider, within the bound.
A program may use at most 192 MiB of HBM per device.

v0:
```python
import math

import jax
import jax.numpy as jnp
from jax import lax
from jax.sharding import PartitionSpec as P

HEADS = 6
GROUPS = 32


EPSILON = 1e-05


def group_norm(values, gain_row, shift_row):
    pixels, channels = values.shape
    grouped = values.reshape(pixels, GROUPS, channels // GROUPS)
    centre = jnp.mean(grouped, axis=(0, 2), keepdims=True)
    spread = jnp.mean(jnp.square(grouped - centre), axis=(0, 2), keepdims=True)
    normal = (grouped - centre) * lax.rsqrt(spread + EPSILON)
    return normal.reshape(pixels, channels) * gain_row + shift_row


def entry_piece(source, gain_row, shift_row):
    return jax.nn.silu(group_norm(source, gain_row, shift_row))


def middle_piece(first_out, gain_row, shift_row, modulate):
    channels = first_out.shape[1]
    normed = group_norm(first_out, gain_row, shift_row)
    return jax.nn.silu(modulate[channels:] + normed * (modulate[:channels] + 1.0))


def contract_rows(left_side, right_side):
    return lax.dot_general(
        left_side, right_side, (((0,), (0,)), ((), ())), preferred_element_type=jnp.float32
    )


def contract_cols(left_side, right_side):
    return lax.dot_general(
        left_side, right_side, (((1,), (1,)), ((), ())), preferred_element_type=jnp.float32
    )


def patches(picture, side_len):
    channels = picture.shape[1]
    padded = jnp.pad(picture.reshape(side_len, side_len, channels), ((1, 1), (1, 1), (0, 0)))
    pieces = [
        padded[row_shift : row_shift + side_len, col_shift : col_shift + side_len, :]
        for row_shift in range(3)
        for col_shift in range(3)
    ]
    return jnp.concatenate(pieces, axis=2).reshape(side_len * side_len, 9 * channels)


def flipped(weight):
    channels = weight.shape[0] // 9
    kernel = weight.reshape(3, 3, channels, weight.shape[1])
    return jnp.transpose(kernel[::-1, ::-1], (0, 1, 3, 2)).reshape(9 * weight.shape[1], channels)


def modulation(embed_row, w_affine, shift_rows):
    scaled = jnp.dot(embed_row[None, :], w_affine, preferred_element_type=jnp.float32)[0]
    return scaled + jnp.concatenate([shift_rows[2], shift_rows[3]])


def qkv_shift(shift_rows):
    return jnp.concatenate([shift_rows[7], jnp.zeros_like(shift_rows[7]), shift_rows[8]])


def split_heads(projected):
    pixels = projected.shape[0]
    channels = projected.shape[1] // 3
    head_width = channels // HEADS
    queries = projected[:, :channels].reshape(pixels, HEADS, head_width)
    key_rows = projected[:, channels : 2 * channels].reshape(pixels, HEADS, head_width)
    value_rows = projected[:, 2 * channels :].reshape(pixels, HEADS, head_width)
    return (queries, key_rows, value_rows, 1.0 / math.sqrt(head_width))


def attend(projected):
    queries, key_rows, value_rows, factor = split_heads(projected)
    pixels = projected.shape[0]
    block_rows = min(512, pixels)
    results = []
    totals = []
    for first_row in range(0, pixels, block_rows):
        scores = (
            jnp.einsum(
                "qhd,khd->hqk",
                queries[first_row : first_row + block_rows],
                key_rows,
                preferred_element_type=jnp.float32,
            )
            * factor
        )
        row_peak = jnp.max(scores, axis=2, keepdims=True)
        exponent = jnp.exp(scores - row_peak)
        summed = jnp.sum(exponent, axis=2, keepdims=True)
        probs_block = (exponent / summed).astype(jnp.bfloat16)
        results.append(
            jnp.einsum("hqk,khd->qhd", probs_block, value_rows, preferred_element_type=jnp.float32)
        )
        totals.append((row_peak + jnp.log(summed))[:, :, 0])
    attended = jnp.concatenate(results, axis=0).reshape(pixels, -1).astype(jnp.bfloat16)
    return (attended, jnp.concatenate(totals, axis=1))


def attend_back(projected, log_totals, grad_attended):
    queries, key_rows, value_rows, factor = split_heads(projected)
    pixels = projected.shape[0]
    grad_heads = grad_attended.reshape(pixels, HEADS, -1)
    block_rows = min(512, pixels)
    grad_keys = jnp.zeros(key_rows.shape, jnp.float32)
    grad_values = jnp.zeros(value_rows.shape, jnp.float32)
    grad_queries = []
    for first_row in range(0, pixels, block_rows):
        query_block = queries[first_row : first_row + block_rows]
        grad_block = grad_heads[first_row : first_row + block_rows]
        scores = (
            jnp.einsum("qhd,khd->hqk", query_block, key_rows, preferred_element_type=jnp.float32)
            * factor
        )
        probs_block = jnp.exp(scores - log_totals[:, first_row : first_row + block_rows, None])
        grad_values = grad_values + jnp.einsum(
            "hqk,qhd->khd",
            probs_block.astype(jnp.bfloat16),
            grad_block,
            preferred_element_type=jnp.float32,
        )
        grad_probs = jnp.einsum(
            "qhd,khd->hqk", grad_block, value_rows, preferred_element_type=jnp.float32
        )
        row_dot = jnp.sum(grad_probs * probs_block, axis=2, keepdims=True)
        grad_scores = (probs_block * (grad_probs - row_dot)).astype(jnp.bfloat16)
        grad_queries.append(
            jnp.einsum("hqk,khd->qhd", grad_scores, key_rows, preferred_element_type=jnp.float32)
            * factor
        )
        grad_keys = (
            grad_keys
            + jnp.einsum(
                "hqk,qhd->khd", grad_scores, query_block, preferred_element_type=jnp.float32
            )
            * factor
        )
    merged = jnp.concatenate(
        [jnp.concatenate(grad_queries, axis=0), grad_keys, grad_values], axis=1
    )
    return merged.reshape(pixels, -1).astype(jnp.bfloat16)


def image_forward(picture, embed_row, weights, side_len):
    gain_all, shifts, w_conv0, w_conv1, w_affine, w_qkv, w_proj = weights
    gain_rows = gain_all.astype(jnp.float32)
    shift_rows = shifts.astype(jnp.float32)
    channels = picture.shape[-1]
    source = picture.reshape(side_len * side_len, channels).astype(jnp.float32)
    entry_act = entry_piece(source, gain_rows[0], shift_rows[0]).astype(jnp.bfloat16)
    first_out = (
        jnp.dot(patches(entry_act, side_len), w_conv0, preferred_element_type=jnp.float32)
        + shift_rows[1]
    )
    modulate = modulation(embed_row, w_affine, shift_rows)
    middle_act = middle_piece(first_out, gain_rows[1], shift_rows[4], modulate).astype(jnp.bfloat16)
    residual = (
        jnp.dot(patches(middle_act, side_len), w_conv1, preferred_element_type=jnp.float32)
        + shift_rows[5]
        + source
    )
    normed = group_norm(residual, gain_rows[2], shift_rows[6]).astype(jnp.bfloat16)
    projected = (
        jnp.dot(normed, w_qkv, preferred_element_type=jnp.float32) + qkv_shift(shift_rows)
    ).astype(jnp.bfloat16)
    attended, log_totals = attend(projected)
    output = (
        jnp.dot(attended, w_proj, preferred_element_type=jnp.float32) + shift_rows[9] + residual
    )
    return (
        output.astype(jnp.bfloat16).reshape(picture.shape),
        (first_out, residual, projected, attended, log_totals),
    )


def image_backward(picture, embed_row, cotangent, kept_state, weights, flipped_pair, side_len):
    gain_all, shifts, w_conv0, w_conv1, w_affine, w_qkv, w_proj = weights
    first_out, residual, projected, attended, log_totals = kept_state
    gain_rows = gain_all.astype(jnp.float32)
    shift_rows = shifts.astype(jnp.float32)
    channels = picture.shape[-1]
    pixels = side_len * side_len
    source = picture.reshape(pixels, channels).astype(jnp.float32)
    grad_out = cotangent.reshape(pixels, channels)
    grad_out_wide = grad_out.astype(jnp.float32)
    grad_proj = contract_rows(attended, grad_out)
    grad_attended = contract_cols(grad_out, w_proj).astype(jnp.bfloat16)
    grad_projected = attend_back(projected, log_totals, grad_attended)
    normed_wide, norm_pull = jax.vjp(group_norm, residual, gain_rows[2], shift_rows[6])
    grad_qkv = contract_rows(normed_wide.astype(jnp.bfloat16), grad_projected)
    grad_normed = contract_cols(grad_projected, w_qkv)
    grad_resid_norm, grad_gain2, grad_shift2 = norm_pull(grad_normed)
    grad_residual = grad_out_wide + grad_resid_norm
    grad_second = grad_residual.astype(jnp.bfloat16)
    modulate = modulation(embed_row, w_affine, shift_rows)
    middle_wide, middle_pull = jax.vjp(
        middle_piece, first_out, gain_rows[1], shift_rows[4], modulate
    )
    grad_conv1 = contract_rows(patches(middle_wide.astype(jnp.bfloat16), side_len), grad_second)
    grad_middle = jnp.dot(
        patches(grad_second, side_len), flipped_pair[1], preferred_element_type=jnp.float32
    )
    grad_first_wide, grad_gain1, grad_shift1, grad_mod_wide = middle_pull(grad_middle)
    grad_first = grad_first_wide.astype(jnp.bfloat16)
    grad_mod = grad_mod_wide.astype(jnp.bfloat16)
    grad_affine = jnp.dot(embed_row[:, None], grad_mod[None, :], preferred_element_type=jnp.float32)
    entry_wide, entry_pull = jax.vjp(entry_piece, source, gain_rows[0], shift_rows[0])
    grad_conv0 = contract_rows(patches(entry_wide.astype(jnp.bfloat16), side_len), grad_first)
    grad_entry = jnp.dot(
        patches(grad_first, side_len), flipped_pair[0], preferred_element_type=jnp.float32
    )
    grad_source, grad_gain0, grad_shift0 = entry_pull(grad_entry)
    grad_input = (grad_residual + grad_source).astype(jnp.bfloat16).reshape(picture.shape)
    mod_sums = grad_mod.astype(jnp.float32)
    qkv_sums = jnp.sum(grad_projected.astype(jnp.float32), axis=0)
    grad_gains = jnp.stack([grad_gain0, grad_gain1, grad_gain2])
    grad_shifts = jnp.stack(
        [
            grad_shift0,
            jnp.sum(grad_first.astype(jnp.float32), axis=0),
            mod_sums[:channels],
            mod_sums[channels:],
            grad_shift1,
            jnp.sum(grad_second.astype(jnp.float32), axis=0),
            grad_shift2,
            qkv_sums[:channels],
            qkv_sums[2 * channels :],
            jnp.sum(grad_out_wide, axis=0),
        ]
    )
    return (
        grad_input,
        (grad_gains, grad_shifts, grad_conv0, grad_conv1, grad_affine, grad_qkv, grad_proj),
    )


def embed_rows(class_table, sigma_table, labels, sigmas):
    summed = class_table[labels].astype(jnp.float32) + sigma_table[sigmas].astype(jnp.float32)
    return jax.nn.silu(summed).astype(jnp.bfloat16)


def run_forward(images, embeds, live_count, weights):
    capacity = images.shape[0]
    side_len = images.shape[1]
    channels = images.shape[-1]
    pixels = side_len * side_len
    outputs_start = jnp.zeros(images.shape, jnp.bfloat16)
    kept_start = (
        jnp.zeros((capacity, pixels, channels), jnp.float32),
        jnp.zeros((capacity, pixels, channels), jnp.float32),
        jnp.zeros((capacity, pixels, 3 * channels), jnp.bfloat16),
        jnp.zeros((capacity, pixels, channels), jnp.bfloat16),
        jnp.zeros((capacity, HEADS, pixels), jnp.float32),
    )

    def loop_step(slot_index, loop_state):
        outputs, kept_state = loop_state
        picture = lax.dynamic_index_in_dim(images, slot_index, 0, keepdims=False)
        embed_row = lax.dynamic_index_in_dim(embeds, slot_index, 0, keepdims=False)
        output, kept_now = image_forward(picture, embed_row, weights, side_len)
        outputs = lax.dynamic_update_index_in_dim(outputs, output, slot_index, 0)
        kept_state = tuple(
            (
                lax.dynamic_update_index_in_dim(buffer, new_value, slot_index, 0)
                for buffer, new_value in zip(kept_state, kept_now)
            )
        )
        return (outputs, kept_state)

    return lax.fori_loop(0, live_count, loop_step, (outputs_start, kept_start))


def run_backward(images, embeds, cotangents, kept_state, live_count, weights, flipped_pair, totals):
    side_len = images.shape[1]
    grads_start = jnp.zeros(images.shape, jnp.bfloat16)

    def loop_step(slot_index, loop_state):
        grads, totals_now = loop_state
        picture = lax.dynamic_index_in_dim(images, slot_index, 0, keepdims=False)
        embed_row = lax.dynamic_index_in_dim(embeds, slot_index, 0, keepdims=False)
        cotangent = lax.dynamic_index_in_dim(cotangents, slot_index, 0, keepdims=False)
        kept_now = tuple(
            (
                lax.dynamic_index_in_dim(buffer, slot_index, 0, keepdims=False)
                for buffer in kept_state
            )
        )
        grad_input, terms = image_backward(
            picture, embed_row, cotangent, kept_now, weights, flipped_pair, side_len
        )
        grads = lax.dynamic_update_index_in_dim(grads, grad_input, slot_index, 0)
        totals_now = tuple((running + added for running, added in zip(totals_now, terms)))
        return (grads, totals_now)

    return lax.fori_loop(0, live_count, loop_step, (grads_start, totals))


def on_device(
    big_images,
    small_images,
    big_labels,
    small_labels,
    big_sigmas,
    small_sigmas,
    loads,
    class_table,
    sigma_table,
    norm_gains,
    biases,
    w_conv0,
    w_conv1,
    w_affine,
    w_qkv,
    w_proj,
    big_cotangent,
    small_cotangent,
):
    weights = (
        lax.all_gather(norm_gains, "shard", axis=1, tiled=True),
        lax.all_gather(biases, "shard", axis=1, tiled=True),
        lax.all_gather(w_conv0, "shard", axis=0, tiled=True),
        lax.all_gather(w_conv1, "shard", axis=0, tiled=True),
        lax.all_gather(w_affine, "shard", axis=0, tiled=True),
        lax.all_gather(w_qkv, "shard", axis=0, tiled=True),
        lax.all_gather(w_proj, "shard", axis=0, tiled=True),
    )
    big_embed = embed_rows(class_table, sigma_table, big_labels, big_sigmas)
    small_embed = embed_rows(class_table, sigma_table, small_labels, small_sigmas)
    big_count = loads[0, 0]
    small_count = loads[0, 1]
    big_output, big_kept = run_forward(big_images, big_embed, big_count, weights)
    small_output, small_kept = run_forward(small_images, small_embed, small_count, weights)
    back_weights = (
        lax.all_gather(norm_gains, "shard", axis=1, tiled=True),
        lax.all_gather(biases, "shard", axis=1, tiled=True),
        lax.all_gather(w_conv0, "shard", axis=0, tiled=True),
        lax.all_gather(w_conv1, "shard", axis=0, tiled=True),
        lax.all_gather(w_affine, "shard", axis=0, tiled=True),
        lax.all_gather(w_qkv, "shard", axis=0, tiled=True),
        lax.all_gather(w_proj, "shard", axis=0, tiled=True),
    )
    flipped_pair = (flipped(back_weights[2]), flipped(back_weights[3]))
    totals = tuple((jnp.zeros(weight_array.shape, jnp.float32) for weight_array in back_weights))
    big_grad, totals = run_backward(
        big_images,
        big_embed,
        big_cotangent,
        big_kept,
        big_count,
        back_weights,
        flipped_pair,
        totals,
    )
    small_grad, totals = run_backward(
        small_images,
        small_embed,
        small_cotangent,
        small_kept,
        small_count,
        back_weights,
        flipped_pair,
        totals,
    )
    grad_gains, grad_shifts, grad_conv0, grad_conv1, grad_affine, grad_qkv, grad_proj = totals
    own_gains, own_shifts, own_conv0, own_conv1, own_affine, own_qkv, own_proj = (
        lax.psum_scatter(
            grad_gains.astype(jnp.bfloat16), "shard", scatter_dimension=1, tiled=True
        ).astype(jnp.float32),
        lax.psum_scatter(
            grad_shifts.astype(jnp.bfloat16), "shard", scatter_dimension=1, tiled=True
        ).astype(jnp.float32),
        lax.psum_scatter(
            grad_conv0.astype(jnp.bfloat16), "shard", scatter_dimension=0, tiled=True
        ).astype(jnp.float32),
        lax.psum_scatter(
            grad_conv1.astype(jnp.bfloat16), "shard", scatter_dimension=0, tiled=True
        ).astype(jnp.float32),
        lax.psum_scatter(
            grad_affine.astype(jnp.bfloat16), "shard", scatter_dimension=0, tiled=True
        ).astype(jnp.float32),
        lax.psum_scatter(
            grad_qkv.astype(jnp.bfloat16), "shard", scatter_dimension=0, tiled=True
        ).astype(jnp.float32),
        lax.psum_scatter(
            grad_proj.astype(jnp.bfloat16), "shard", scatter_dimension=0, tiled=True
        ).astype(jnp.float32),
    )
    out_gains, out_shifts, out_conv0, out_conv1, out_affine, out_qkv, out_proj = (
        lax.psum(own_gains.astype(jnp.bfloat16), "rep").astype(jnp.float32),
        lax.psum(own_shifts.astype(jnp.bfloat16), "rep").astype(jnp.float32),
        lax.psum(own_conv0.astype(jnp.bfloat16), "rep").astype(jnp.float32),
        lax.psum(own_conv1.astype(jnp.bfloat16), "rep").astype(jnp.float32),
        lax.psum(own_affine.astype(jnp.bfloat16), "rep").astype(jnp.float32),
        lax.psum(own_qkv.astype(jnp.bfloat16), "rep").astype(jnp.float32),
        lax.psum(own_proj.astype(jnp.bfloat16), "rep").astype(jnp.float32),
    )
    return (
        big_output,
        small_output,
        big_grad,
        small_grad,
        out_gains,
        out_shifts,
        out_conv0,
        out_conv1,
        out_affine,
        out_qkv,
        out_proj,
    )


def solution(mesh):
    return jax.shard_map(
        on_device,
        mesh=mesh,
        in_specs=(
            P(("shard", "rep"), None, None, None),
            P(("shard", "rep"), None, None, None),
            P(("shard", "rep")),
            P(("shard", "rep")),
            P(("shard", "rep")),
            P(("shard", "rep")),
            P(("shard", "rep"), None),
            P(),
            P(),
            P(None, "shard"),
            P(None, "shard"),
            P("shard", None),
            P("shard", None),
            P("shard", None),
            P("shard", None),
            P("shard", None),
            P(("shard", "rep"), None, None, None),
            P(("shard", "rep"), None, None, None),
        ),
        out_specs=(
            P(("shard", "rep"), None, None, None),
            P(("shard", "rep"), None, None, None),
            P(("shard", "rep"), None, None, None),
            P(("shard", "rep"), None, None, None),
            P(None, "shard"),
            P(None, "shard"),
            P("shard", None),
            P("shard", None),
            P("shard", None),
            P("shard", None),
            P("shard", None),
        ),
        check_vma=False,
    )
```

profile of v0, /device:TPU:0, one launch (start us, length us, event | category | flops | bytes accessed | tf_op | source)
XLA Modules:
  0.0 928.2 jit_solution(15337743548138823328)
XLA Ops:
  12.0 10.7 %all-gather = bf16[8,48,10]{1,2,0:T(8,128)(2,1)S(1)} all-gather(bf16[1,48,10]{1,2,0:T(8,128)(2,1)} %bitcast.711), channel_id=1, replica_groups=mesh['shard'=8,'rep'=4] {'shard'}, dimensions={0}, use_global_device_ids=true | all-gather | bytes 8640 | tf_op jit(solution)/shard_map/all_gather | solution.py:330
  26.8 8.7 all-gather.1
  40.8 8.6 all_gather.34
  52.3 3.2 pad_slice_fusion.32
  60.7 2.9 copy-done.96
  71.1 14.3 %all_gather.33 = bf16[384,1152]{1,0:T(8,128)(2,1)} all-gather(bf16[48,1152]{1,0:T(8,128)(2,1)S(1)} %copy-done.88), channel_id=1, replica_groups=mesh['shard'=8,'rep'=4] {'shard'}, dimensions={0}, use_global_device_ids=true | all-gather | bytes 995328 | tf_op jit(solution)/shard_map/all_gather | solution.py:334
  90.7 3.8 add_reduce_fusion.1
  102.5 3.4 fusion.176
  121.1 5.6 while.126
  137.6 6.1 add_reduce_fusion
  151.8 5.1 fusion.177
  159.4 5.0 add_convert_fusion.4
  188.3 6.5 fusion.90
  196.9 3.6 fusion.89
  221.0 4.5 multiply_reduce_fusion.1
  225.6 4.7 multiply_convert_fusion.1
  230.3 5.7 fusion.88
  238.4 3.0 fusion.197
  241.4 6.4 multiply_reduce_fusion
  250.6 10.3 %multiply_convert_fusion = bf16[6,512,1024]{2,1,0:T(8,128)(2,1)} fusion(f32[6,512,1024]{2,1,0:T(8,128)} %get-tuple-element.4368, f32[6,512,1024]{2,1,0:T(8,128)S(1)} %fusion.197, f32[6,512]{1,0:T(8,128)S(1)} %get-tuple-element.4367, f32[6,512]{1,0:T(8,128)S(1)} %copy-done.71), kind=kLoop, calls=%fused_computation.78 | loop fusion | flops 15728640 | bytes 31481856 | tf_op jit(solution)/shard_map/while/body/convert_element_type | solution.py:136
  260.9 5.8 fusion.87
  266.7 4.0 multiply_bitcast_fusion
  270.8 3.8 add_bitcast_fusion
  287.2 3.6 multiply_reduce_fusion.6
  307.4 3.6 reverse_bitcast_fusion.1
  311.0 5.9 copy.142
  318.8 3.4 fusion.202
  325.2 3.5 multiply_reduce_fusion.20
  332.3 4.9 fusion.201
  341.5 5.8 copy.143
  350.2 4.3 fusion.127
  397.2 6.8 multiply_reduce_fusion.5
  408.2 5.8 fusion.200
  431.8 9.2 fusion.199
  446.1 3.9 fusion.198
  491.6 23.6 %while.128 = (s32[]{:T(128)}, bf16[1,16,16,384]{3,2,1,0:T(8,128)(2,1)}, f32[3,384]{1,0:T(4,128)}, f32[10,384]{1,0:T(8,128)}, f32[3456,384]{1,0:T(8,128)}, /*inde...) while((s32[]{:T(128)}, ...), condition=%wide.wide.region_116.117_spmd.clone, body=%wide.wide.region_115.116_spmd.clone.sunk | while | flops 82781312 | bytes 163194928 | solution.py:305
  501.5 3.8 add.2633
  519.0 4.3 convert_element_type.1310
  523.4 4.3 convert_element_type.1312
  532.1 87.8 %reduce-scatter.18.cloned.1.call-done = bf16[48,1152]{1,0:T(8,128)(2,1)} async-done(((bf16[384,1152]{1,0:T(8,128)(2,1)}), bf16[48,1152]{1,0:T(8,128)(2,1)}) %reduce-scatter.18.cloned.1.call-update) | async-done | bytes 110608 | tf_op jit(solution)/shard_map/reduce_scatter | solution.py:391
  619.9 40.2 %reduce-scatter.16.cloned.1.call-done = bf16[96,768]{1,0:T(8,128)(2,1)} async-done(((bf16[768,768]{1,0:T(8,128)(2,1)}), bf16[96,768]{1,0:T(8,128)(2,1)}) %reduce-scatter.16.cloned.1.call-update) | async-done | bytes 147472 | tf_op jit(solution)/shard_map/reduce_scatter | solution.py:388
  660.2 47.1 %reduce-scatter.12.cloned.1.call-done = bf16[432,384]{1,0:T(8,128)(2,1)} async-done(((bf16[3456,384]{1,0:T(8,128)(2,1)}), bf16[432,384]{1,0:T(8,128)(2,1)}) %reduce-scatter.12.cloned.1.call-update) | async-done | bytes 331792 | tf_op jit(solution)/shard_map/reduce_scatter | solution.py:382
  707.3 47.6 %reduce-scatter.14.cloned.1.call-done = bf16[432,384]{1,0:T(8,128)(2,1)} async-done(((bf16[3456,384]{1,0:T(8,128)(2,1)}), bf16[432,384]{1,0:T(8,128)(2,1)}) %reduce-scatter.14.cloned.1.call-update) | async-done | bytes 331792 | tf_op jit(solution)/shard_map/reduce_scatter | solution.py:385
  754.9 36.0 %reduce-scatter.22.cloned.1.call-done = bf16[48,3]{1,0:T(8,128)(2,1)} async-done(((bf16[384,3]{1,0:T(8,128)(2,1)}), bf16[48,3]{1,0:T(8,128)(2,1)}) %reduce-scatter.22.cloned.1.call-update) | async-done | bytes 304
  791.7 35.3 %reduce-scatter.24.cloned.1.call-done = bf16[48,10]{1,0:T(8,128)(2,1)} async-done(((bf16[384,10]{1,0:T(8,128)(2,1)}), bf16[48,10]{1,0:T(8,128)(2,1)}) %reduce-scatter.24.cloned.1.call-update) | async-done | bytes 976
  827.8 35.6 %reduce-scatter.20.cloned.1.call-done = bf16[48,384]{1,0:T(8,128)(2,1)} async-done(((bf16[384,384]{1,0:T(8,128)(2,1)}), bf16[48,384]{1,0:T(8,128)(2,1)}) %reduce-scatter.20.cloned.1.call-update) | async-done | bytes 36880 | tf_op jit(solution)/shard_map/reduce_scatter | solution.py:394
  863.4 21.0 %all-reduce.18 = (bf16[3,48]{1,0:T(4,128)(2,1)S(1)}, bf16[10,48]{1,0:T(8,128)(2,1)S(1)}, bf16[48,384]{1,0:T(8,128)(2,1)S(1)}) all-reduce(bf16[3,48]{1,0:T(4,128)(2,1)S(1)} %copy.156, bf16[10,48]{1,0:T(8,128)(2,1)S(1)} %copy.158, bf16[48,384]{1,0:T(8,128)(2,1)} %reduce-scatter.20.cloned.1.call-done), channel_id=1, replica_groups=mesh['shard'=8,'rep'=4] {'rep'}, use_global_device_ids=true, to_apply=%region_118.119 | all-reduce | flops 19056 | bytes 76224 | tf_op jit(solution)/shard_map/psum | solution.py:399
  886.3 30.0 %all-reduce.22.cloned.1.call-done = (bf16[432,384]{1,0:T(8,128)(2,1)}, bf16[432,384]{1,0:T(8,128)(2,1)}, bf16[96,768]{1,0:T(8,128)(2,1)}, bf16[48,1152]{1,0:T(8,128)(2,1)}) async-done(((bf16[432,384]{1,0:T(8,128)(2,1)}, bf16[432,384]{1,0:T(8,128)(2,1)}, bf16[96,768]{1,0:T(8,128)(2,1)}, bf16[48,1152]{1,0:T(8,128)(2,1)}), (bf16[432,384]{1,0:T(8,128)(2,1)}, bf16[432,384]{1,0:T(8,128)(2,1)}, ...) | async-done | bytes 921616 | tf_op jit(solution)/shard_map/psum | solution.py:401
  (895 shorter events, 321.6 us)
Async XLA Ops:
  7.2 79.7 %all-gather.6.cloned.1.call-start = ((), (), s32[]{:S(2)}) async-start(), calls=%async_computation.7 | async-start | bytes 1327104 | tf_op jit(solution)/shard_map/all_gather | solution.py:333
  7.9 82.8 %all-gather.8.cloned.1.call-start = ((), (), s32[]{:S(2)}) async-start(), calls=%async_computation.8 | async-start | bytes 2985984 | tf_op jit(solution)/shard_map/all_gather | solution.py:331
  8.7 93.8 %all-gather.10.cloned.1.call-start = ((), (), s32[]{:S(2)}) async-start(), calls=%async_computation.9 | async-start | bytes 2985984 | tf_op jit(solution)/shard_map/all_gather | solution.py:332
  9.4 610.5 %reduce-scatter.18.cloned.1.call-start = ((), (), s32[]{:S(2)}) async-start(), calls=%async_computation.13 | async-start | bytes 995328 | tf_op jit(solution)/shard_map/reduce_scatter | solution.py:391
  23.4 32.6 %copy-start.97 = (f32[384]{0:T(512)}, f32[384]{0:T(512)S(1)}, u32[]{:S(2)}) copy-start(f32[384]{0:T(512)S(1)} %get-tuple-element.3942) | copy-start | bytes 4612
  23.4 71.9 %copy-start.77 = (f32[384]{0:T(512)}, f32[384]{0:T(512)S(1)}, u32[]{:S(2)}) copy-start(f32[384]{0:T(512)S(1)} %get-tuple-element.3940) | copy-start | bytes 4612
  23.5 71.9 %copy-start.93 = (f32[384]{0:T(512)}, f32[384]{0:T(512)S(1)}, u32[]{:S(2)}) copy-start(f32[384]{0:T(512)S(1)} %get-tuple-element.3941) | copy-start | bytes 4612
  25.4 13.1 %copy-start.129 = (f32[384]{0:T(512)}, f32[384]{0:T(512)S(1)}, u32[]{:S(2)}) copy-start(f32[384]{0:T(512)S(1)} %sub.936) | copy-start | bytes 4612
  26.6 9.7 %copy-start.164 = (f32[32]{0:T(128)}, f32[32]{0:T(128)S(1)}, u32[]{:S(2)}) copy-start(f32[32]{0:T(128)S(1)} %reduce_sum.1486) | copy-start | bytes 388
  26.8 11.6 %copy-start.154 = (f32[384]{0:T(512)}, f32[384]{0:T(512)S(1)}, u32[]{:S(2)}) copy-start(f32[384]{0:T(512)S(1)} %mul.2551) | copy-start | bytes 4612
  36.3 19.8 %copy-start.105 = (f32[384]{0:T(512)}, f32[384]{0:T(512)S(1)}, u32[]{:S(2)}) copy-start(f32[384]{0:T(512)S(1)} %get-tuple-element.3947) | copy-start | bytes 4612
  36.3 112.7 %copy-start.72 = (f32[384]{0:T(512)}, f32[384]{0:T(512)S(1)}, u32[]{:S(2)}) copy-start(f32[384]{0:T(512)S(1)} %get-tuple-element.3946) | copy-start | bytes 4612
  37.4 12.0 %copy-start.4 = (bf16[1,32,32,384]{3,2,1,0:T(8,128)(2,1)S(1)}, bf16[1,32,32,384]{3,2,1,0:T(8,128)(2,1)}, u32[]{:S(2)}) copy-start(bf16[1,32,32,384]{3,2,1,0:T(8,128)(2,1)} %param.26) | copy-start | bytes 2359300
  49.4 35.9 %copy-start.37 = (bf16[384,384]{1,0:T(8,128)(2,1)}, bf16[384,384]{1,0:T(8,128)(2,1)S(1)}, u32[]{:S(2)}) copy-start(bf16[384,384]{1,0:T(8,128)(2,1)S(1)} %all_gather.34) | copy-start | bytes 884740
  57.2 8.5 copy-start.178
  57.2 9.0 copy-start.177
  90.1 8.6 copy-start.107
  90.1 8.6 copy-start.135
  151.8 7.6 copy-start.110
  188.3 8.4 copy-start.25
  188.3 8.6 copy-start.64
  188.3 8.6 copy-start.85
  188.3 8.6 copy-start.120
  216.1 14.2 %copy-start.42 = (bf16[1024,384]{0,1:T(8,128)(2,1)}, bf16[1024,384]{0,1:T(8,128)(2,1)S(1)}, u32[]{:S(2)}) copy-start(bf16[1024,384]{0,1:T(8,128)(2,1)S(1)} %copy.139) | copy-start | bytes 2359300
  250.6 10.3 %copy-start.43 = (bf16[1024,384]{0,1:T(8,128)(2,1)S(1)}, bf16[1024,384]{0,1:T(8,128)(2,1)}, u32[]{:S(2)}) copy-start(bf16[1024,384]{0,1:T(8,128)(2,1)} %copy-done.42) | copy-start | bytes 2359300
  250.6 20.1 %slice-start.6 = ((s8[12582912]{0:T(1024)(128)(4,1)}), s8[4194304]{0:T(1024)(128)(4,1)S(1)}, s32[]{:S(2)}) async-start(s8[12582912]{0:T(1024)(128)(4,1)} %bitcast.548), calls=%async_computation.24 | async-start | bytes 8388608
  250.6 20.1 %slice-start.7 = ((s8[12582912]{0:T(1024)(128)(4,1)}), s8[4194304]{0:T(1024)(128)(4,1)S(1)}, s32[]{:S(2)}) async-start(s8[12582912]{0:T(1024)(128)(4,1)} %bitcast.548), calls=%async_computation.25 | async-start | bytes 8388608
  260.9 9.8 %slice-start.8 = ((s8[12582912]{0:T(1024)(128)(4,1)}), s8[4194304]{0:T(1024)(128)(4,1)S(1)}, s32[]{:S(2)}) async-start(s8[12582912]{0:T(1024)(128)(4,1)} %bitcast.548), calls=%async_computation.26 | async-start | bytes 8388608
  274.5 10.2 %copy-start.67 = (bf16[512,6,64]{0,2,1:T(8,128)(2,1)S(1)}, bf16[512,6,64]{0,2,1:T(8,128)(2,1)}, u32[]{:S(2)}) copy-start(bf16[512,6,64]{0,2,1:T(8,128)(2,1)} %fusion.88) | copy-start | bytes 1179652
  341.5 8.7 copy-start.14
  350.2 8.5 copy-start.180
  350.2 9.1 copy-start.186
  350.2 9.7 %copy-start.179 = (f32[384]{0:T(512)S(1)}, f32[384]{0:T(512)}, u32[]{:S(2)}) copy-start(f32[384]{0:T(512)} %get-tuple-element.5835) | copy-start | bytes 4612
  350.2 10.2 %copy-start.185 = (f32[384]{0:T(512)S(1)}, f32[384]{0:T(512)}, u32[]{:S(2)}) copy-start(f32[384]{0:T(512)} %get-tuple-element.5836) | copy-start | bytes 4612
  350.2 10.8 %copy-start.184 = (f32[384]{0:T(512)S(1)}, f32[384]{0:T(512)}, u32[]{:S(2)}) copy-start(f32[384]{0:T(512)} %get-tuple-element.3910) | copy-start | bytes 4612
  350.2 11.0 %copy-start.170 = (f32[32]{0:T(128)S(1)}, f32[32]{0:T(128)}, u32[]{:S(2)}) copy-start(f32[32]{0:T(128)} %reduce_sum.1507) | copy-start | bytes 388
  350.2 12.3 %copy-start.133 = (f32[384]{0:T(512)S(1)}, f32[384]{0:T(512)}, u32[]{:S(2)}) copy-start(f32[384]{0:T(512)} %copy-done.131) | copy-start | bytes 4612
  363.4 24.3 %copy-start.19 = (bf16[1,32,32,384]{3,2,1,0:T(8,128)(2,1)S(1)}, bf16[1,32,32,384]{3,2,1,0:T(8,128)(2,1)}, u32[]{:S(2)}) copy-start(bf16[1,32,32,384]{3,2,1,0:T(8,128)(2,1)} %param.42) | copy-start | bytes 2359300
  408.2 11.4 %copy-start.17 = (f32[1,1024,384]{2,1,0:T(8,128)S(1)}, f32[1,1024,384]{2,1,0:T(8,128)}, u32[]{:S(2)}) copy-start(f32[1,1024,384]{2,1,0:T(8,128)} %get-tuple-element.3493) | copy-start | bytes 4718596
  450.0 22.1 %copy-start.21 = (f32[1024,384]{1,0:T(8,128)}, f32[1024,384]{1,0:T(8,128)S(1)}, u32[]{:S(2)}) copy-start(f32[1024,384]{1,0:T(8,128)S(1)} %fusion.198) | copy-start | bytes 4718596
  460.5 15.1 %copy-start.181 = (f32[1,384]{1,0:T(1,128)S(1)}, f32[1,384]{1,0:T(1,128)}, u32[]{:S(2)}) copy-start(f32[1,384]{1,0:T(1,128)} %reshape.4104) | copy-start | bytes 4612
  517.8 142.4 %reduce-scatter.16.cloned.1.call-start = ((), (), s32[]{:S(2)}) async-start(), calls=%async_computation.12 | async-start | bytes 1327104 | tf_op jit(solution)/shard_map/reduce_scatter | solution.py:388
  519.0 188.3 %reduce-scatter.12.cloned.1.call-start = ((), (), s32[]{:S(2)}) async-start(), calls=%async_computation.10 | async-start | bytes 2985984 | tf_op jit(solution)/shard_map/reduce_scatter | solution.py:382
  523.4 231.5 %reduce-scatter.14.cloned.1.call-start = ((), (), s32[]{:S(2)}) async-start(), calls=%async_computation.11 | async-start | bytes 2985984 | tf_op jit(solution)/shard_map/reduce_scatter | solution.py:385
  527.8 263.2 %reduce-scatter.22.cloned.1.call-start = ((), (), s32[]{:S(2)}) async-start(), calls=%async_computation.15 | async-start | bytes 110592
  529.3 297.7 %reduce-scatter.24.cloned.1.call-start = ((), (), s32[]{:S(2)}) async-start(), calls=%async_computation.16 | async-start | bytes 110592
  530.2 333.2 %reduce-scatter.20.cloned.1.call-start = ((), (), s32[]{:S(2)}) async-start(), calls=%async_computation.14 | async-start | bytes 331776 | tf_op jit(solution)/shard_map/reduce_scatter | solution.py:394
  532.1 384.2 %all-reduce.22.cloned.1.call-start = ((), (), s32[]{:S(2)}) async-start(), calls=%async_computation.17 | async-start | bytes 1843200 | tf_op jit(solution)/shard_map/psum | solution.py:401
  (154 other events, 515.1 us)
Sparse Core Ops, SparseCore 0:
  9.9 26.8 all-gather.5
  38.6 30.2 all-gather.7
  70.8 31.3 all-gather.9
  517.9 101.9 reduce-scatter.17
  623.3 36.7 reduce-scatter.15
  663.5 43.7 reduce-scatter.11
  711.1 43.7 reduce-scatter.13
  758.5 32.4 reduce-scatter.21
  794.6 32.4 reduce-scatter.23
  830.5 32.8 reduce-scatter.19
  866.1 50.1 all-reduce.21
where the time goes:
time: 939 us; the launch traced here: 928 us
  waiting for transfers between devices  362 us (39%)
  local copies, waits for them, and re-layouts  202 us (22%)
  matrix products  148 us (16%)
  other arithmetic  128 us (14%)
  blocking collectives  63.3 us (7%)
  between operations  19.5 us (2%)
    reduce_scatter x1, waiting for transfers between devices, on_device(): lax.psum_scatter(grad_qkv.astype(jnp.bfloat16), 'shard', scatter_dimensio...  87.8 us
    unnamed x13, waiting for transfers between devices  73.5 us
    unnamed x414, local copies, waits for them, and re-layouts  51.7 us
    reduce_scatter x1, waiting for transfers between devices, on_device(): lax.psum_scatter(grad_conv1.astype(jnp.bfloat16), 'shard', scatter_dimens...  47.6 us
    reduce_scatter x1, waiting for transfers between devices, on_device(): lax.psum_scatter(grad_conv0.astype(jnp.bfloat16), 'shard', scatter_dimens...  47.1 us
    reduce_scatter x1, waiting for transfers between devices, on_device(): lax.psum_scatter(grad_affine.astype(jnp.bfloat16), 'shard', scatter_dimen...  40.2 us
    reduce_scatter x1, waiting for transfers between devices, on_device(): lax.psum_scatter(grad_proj.astype(jnp.bfloat16), 'shard', scatter_dimensi...  35.6 us
    dot_general x8, matrix products, contract_rows(): lax.dot_general(left_side, right_side, (((0,), (0,)), ((), ())), preferre...  32.5 us
  transfers between devices with their start and end apart: 11, of which 8 were waited for; matrix products, arithmetic and copies ran while one was open for 6% of the time, Pallas kernels for 0%

commit v1 on v0

v1 whole, which is shorter than its diff:
```python
import math
import types

import jax
import jax.numpy as jnp
from jax import lax
from jax.experimental import pallas as pl
from jax.experimental.pallas import tpu as pltpu
from jax.sharding import PartitionSpec as P

HEADS = 6
GROUPS = 32
EPSILON = 1e-05
BF = jnp.bfloat16
F32 = jnp.float32
BLK = 256


def mm(left, right, lc=1, rc=0):
    return lax.dot_general(left, right, (((lc,), (rc,)), ((), ())), preferred_element_type=F32)


def fold(values):
    rows, cols = values.shape
    return jnp.sum(values.reshape(rows // 8, 8, cols), axis=0)


def total(folded):
    return jnp.sum(folded, axis=0, keepdims=True)


def sigmoid(z):
    return 0.5 * jnp.tanh(0.5 * z) + 0.5


class Seg:
    def __init__(self, index, row, pad, side):
        self.index, self.row, self.pad, self.side = index, row, pad, side
        self.pixels = side * side


def make_segs(sides):
    segs, row, pad = [], 0, 0
    for index, side in enumerate(sides):
        segs.append(Seg(index, row, pad + side, side))
        row += side * side
        pad += side * side + 2 * side
    return segs, row, pad


def each_block(seg, body, carry, ticks=None):
    count = seg.pixels // BLK
    due = {n: act for (image, n), act in (ticks or {}).items() if image == seg.index}
    if count == 1:
        for act in due.values():
            act()
        return body(0, carry)

    def step(i, c):
        for n, act in due.items():
            pl.when(i == n)(act)
        return body(pl.multiple_of(i * BLK, BLK), c)

    return lax.fori_loop(0, count, step, carry)


def rows_at(start, size=BLK):
    return pl.ds(pl.multiple_of(start, 16) if not isinstance(start, int) else start, size)


def three_parts(value):
    high = value.astype(BF).astype(F32)
    mid = (value - high).astype(BF).astype(F32)
    return [high, mid, (value - high - mid).astype(BF).astype(F32)]


def group_mean(rows, group_ref):
    count, channels = len(rows), rows[0].shape[1]
    parts = []
    for row in rows:
        parts += three_parts(row)
    padded = -(-3 * count // 16) * 16
    parts.append(jnp.zeros((padded - 3 * count, channels), F32))
    stacked = jnp.concatenate(parts, axis=0).astype(BF)
    sums = mm(stacked, group_ref[...]) * (GROUPS / channels)
    return [total(sums[3 * i : 3 * i + 3]) for i in range(count)]


def shift_pair(values, side):
    rows = values.shape[0]
    place = lax.broadcasted_iota(jnp.int32, (rows, 1), 0) % side
    before = jnp.where(place == 0, 0.0, pltpu.roll(values, 1, 0))
    after = jnp.where(place == side - 1, 0.0, pltpu.roll(values, rows - 1, 0))
    return before, after


class Moments:
    @staticmethod
    def start(channels):
        return (jnp.zeros((1, channels), F32), jnp.zeros((8, channels), F32), jnp.zeros((8, channels), F32))

    @staticmethod
    def add(carry, values, first):
        about, once, twice = carry
        about = jnp.where(first, values[0:1], about)
        off = values - about
        return (about, once + fold(off), twice + fold(off * off))


def norm_stats(segs, sums, group_ref):
    means, variances = [], []
    for seg, (about, once, twice) in zip(segs, sums):
        off = total(once) * (1.0 / seg.pixels)
        means.append(about + off)
        variances.append(jnp.maximum(total(twice) * (1.0 / seg.pixels) - off * off, 0.0))
    centres = group_mean(means, group_ref)
    spreads = group_mean(
        [v + (m - c) * (m - c) for v, m, c in zip(variances, means, centres)], group_ref
    )
    return [(c, lax.rsqrt(s + EPSILON)) for c, s in zip(centres, spreads)]


def norm_back_terms(segs, sums, stats, scales, group_ref):
    rows = []
    for seg, (s0, s1), scale in zip(segs, sums, scales):
        rows += [scale * s0 * (1.0 / seg.pixels), scale * s1 * (1.0 / seg.pixels)]
    means = group_mean(rows, group_ref)
    result = []
    for i, ((centre, inverse), scale) in enumerate(zip(stats, scales)):
        result.append((inverse * scale, inverse * means[2 * i], inverse * inverse * means[2 * i + 1]))
    return result


def store_triple(ref, seg, start, values, backward):
    channels = values.shape[1]
    before, after = shift_pair(values, seg.side)
    low, high = (after, before) if backward else (before, after)
    at = rows_at(seg.pad + start)
    ref[at, 0:channels] = low.astype(BF)
    ref[at, channels : 2 * channels] = values.astype(BF)
    ref[at, 2 * channels : 3 * channels] = high.astype(BF)


def zero_pads(ref, segs):
    columns = ref.shape[1]
    for seg in segs:
        ref[seg.pad - seg.side : seg.pad, :] = jnp.zeros((seg.side, columns), ref.dtype)
        ref[seg.pad + seg.pixels : seg.pad + seg.pixels + seg.side, :] = jnp.zeros((seg.side, columns), ref.dtype)


def conv_block(triple, weight, seg, start):
    width = triple.shape[1]
    out = None
    for a in range(3):
        term = mm(triple[rows_at(seg.pad + start + (a - 1) * seg.side), :], weight[a * width : (a + 1) * width, :])
        out = term if out is None else out + term
    return out


def conv_back_block(triple, crossed, seg, start):
    width = triple.shape[1]
    third = width // 3
    out = None
    for a in range(3):
        term = mm(
            triple[rows_at(seg.pad + start - (a - 1) * seg.side), :], crossed[a * third : (a + 1) * third, :], 1, 1
        )
        out = term if out is None else out + term
    return out


def cross_weight(source, target):
    channels = source.shape[1]

    def step(a, carry):
        for b in range(3):
            target[pl.ds(pl.multiple_of(a * channels, channels), channels), b * channels : (b + 1) * channels] = source[
                pl.ds(pl.multiple_of((3 * a + b) * channels, channels), channels), :
            ]
        return carry

    lax.fori_loop(0, 3, step, 0)


def conv_weight_grad(kept, triple, segs, store, columns):
    channels = kept.shape[1]
    first_col, last_col = columns
    width = last_col - first_col
    for a in range(3):
        out = None
        for seg in segs:
            first = seg.pad + (a - 1) * seg.side
            span = slice(seg.pad, seg.pad + seg.pixels)
            if width == channels:
                right = triple[span, :]
            else:
                right = jnp.concatenate(
                    [triple[span, b * channels + first_col : b * channels + last_col] for b in range(3)], axis=1
                )
            term = mm(kept[first : first + seg.pixels, :], right, 0, 0)
            out = term if out is None else out + term
        for b in range(3):
            store((3 * a + b) * channels, first_col, out[:, b * width : (b + 1) * width])


def attention(seg, block, keyvalue, qkv_t, datt_t, dkv):
    channels = datt_t.shape[0]
    head = channels // HEADS
    pair = 2 * head
    pixels = seg.pixels
    span = pl.ds(seg.row, pixels)
    place = lax.broadcasted_iota(jnp.int32, (pair, 1), 0)

    def heads(index, carry):
        ro = pl.multiple_of(index * pair, pair)
        keys = keyvalue[span, pl.ds(channels + ro, pair)]
        values = keyvalue[span, pl.ds(2 * channels + ro, pair)]

        def queries(step, inner):
            r = seg.row + step * block
            at = pl.ds(pl.multiple_of(r, block) if not isinstance(r, int) else r, block)
            q_pair = qkv_t[pl.ds(ro, pair), at]
            d_pair = datt_t[pl.ds(ro, pair), at]
            dk, dv = 0, 0
            for h in range(2):
                mine = (place < head) if h == 0 else (place >= head)
                q = jnp.where(mine, q_pair, 0).astype(BF)
                scores = mm(keys, q)
                peak = jnp.max(scores, axis=0, keepdims=True)
                probs = jnp.exp(scores - peak)
                inverse = 1.0 / jnp.sum(probs, axis=0, keepdims=True)
                probs_b = probs.astype(BF)
                k_t = qkv_t[pl.ds(channels + ro + h * head, head), span]
                v_t = qkv_t[pl.ds(2 * channels + ro + h * head, head), span]
                out_t = mm(v_t, probs_b) * inverse
                d_att = (jnp.where(mine, d_pair, 0).astype(F32) * inverse).astype(BF)
                dots = jnp.sum(d_att[h * head : (h + 1) * head].astype(F32) * out_t, axis=0, keepdims=True)
                d_probs = mm(values, d_att)
                d_scores = (probs * (d_probs - dots)).astype(BF)
                qkv_t[pl.ds(ro + h * head, head), at] = out_t.astype(BF)
                datt_t[pl.ds(ro + h * head, head), at] = (mm(k_t, d_scores) * (1.0 / math.sqrt(head))).astype(BF)
                dk = dk + mm(d_scores, q, 1, 1)
                dv = dv + mm(probs_b, d_att, 1, 1)
            if isinstance(step, int):
                dkv[span, pl.ds(ro, pair)] = dk
                dkv[span, pl.ds(channels + ro, pair)] = dv
            else:
                first = step == 0
                dkv[span, pl.ds(ro, pair)] = dk + jnp.where(first, 0.0, dkv[span, pl.ds(ro, pair)])
                dkv[span, pl.ds(channels + ro, pair)] = dv + jnp.where(first, 0.0, dkv[span, pl.ds(channels + ro, pair)])
            return inner

        if pixels == block:
            return queries(0, carry)
        return lax.fori_loop(0, pixels // block, queries, carry)

    lax.fori_loop(0, HEADS // 2, heads, 0)


def block_body(sides, r, hook=lambda name: None, ticks=lambda name: None):
    segs, rows_all, pad_all = make_segs(sides)
    ch = r.x.shape[1]
    x, g, out, grad = r.x, r.g, r.out, r.grad
    triple, kept0, kept1 = r.triple, r.kept0, r.kept1
    y0, res, wide = r.y0, r.res, r.wide
    gain = lambda i: r.params[i : i + 1, :]
    shift_row = lambda i: r.params[3 + i : 4 + i, :]
    groups = r.groups
    for ref in (triple, kept0, kept1):
        zero_pads(ref, segs)
    lane = lax.broadcasted_iota(jnp.int32, (ch, ch), 1)
    sub = lax.broadcasted_iota(jnp.int32, (ch, ch), 0)
    width = ch // GROUPS
    diff = sub // width - lane // width
    groups[...] = jnp.where(diff == 0, 1.0, 0.0).astype(BF)

    sums = []
    for seg in segs:
        def go(start, carry, seg=seg):
            return Moments.add(carry, x[rows_at(seg.row + start), :].astype(F32), start == 0)
        sums.append(each_block(seg, go, Moments.start(ch)))
    hook("shifts")
    stats0 = norm_stats(segs, sums, groups)
    for seg, (centre, inverse) in zip(segs, stats0):
        scale, shift = inverse * gain(0), shift_row(0)
        def go(start, carry, seg=seg, centre=centre, scale=scale, shift=shift):
            z = (x[rows_at(seg.row + start), :].astype(F32) - centre) * scale + shift
            a0 = z * sigmoid(z)
            store_triple(triple, seg, start, a0, False)
            kept0[rows_at(seg.pad + start), :] = a0.astype(BF)
            return carry
        each_block(seg, go, 0)

    hook("w0")
    sums = []
    for seg in segs:
        def go(start, carry, seg=seg):
            value = conv_block(triple, r.w0, seg, start) + shift_row(1)
            y0[rows_at(seg.row + start), :] = value
            return Moments.add(carry, value, start == 0)
        sums.append(each_block(seg, go, Moments.start(ch), ticks("conv0")))
    hook("conv0")
    stats1 = norm_stats(segs, sums, groups)
    hook("affine")
    mod = r.mod
    scales1, consts1 = [], []
    for seg, (centre, inverse) in zip(segs, stats1):
        stretch = mod[seg.index : seg.index + 1, :ch] + shift_row(2) + 1.0
        offset = mod[seg.index : seg.index + 1, ch:] + shift_row(3)
        scales1.append(gain(1) * stretch)
        shift = shift_row(4) * stretch + offset
        consts1.append((stretch, centre, inverse, inverse * scales1[-1], shift))
        _, _, _, scale, _ = consts1[-1]
        def go(start, carry, seg=seg, centre=centre, scale=scale, shift=shift):
            z = (y0[rows_at(seg.row + start), :] - centre) * scale + shift
            a1 = z * sigmoid(z)
            store_triple(triple, seg, start, a1, False)
            kept1[rows_at(seg.pad + start), :] = a1.astype(BF)
            return carry
        each_block(seg, go, 0)

    hook("w1")
    sums = []
    for seg in segs:
        def go(start, carry, seg=seg):
            at = rows_at(seg.row + start)
            value = conv_block(triple, r.w1, seg, start) + shift_row(5) + x[at, :].astype(F32)
            res[at, :] = value
            return Moments.add(carry, value, start == 0)
        sums.append(each_block(seg, go, Moments.start(ch), ticks("conv1")))
    stats2 = norm_stats(segs, sums, groups)

    hook("wqkv")
    hook("wproj")
    a2, kv, qkv_t, datt_t = r.a2, r.dqkv, r.qkv_t, r.datt_t
    w_qkv, w_proj = r.wqkv, r.wproj
    for seg, (centre, inverse) in zip(segs, stats2):
        scale, shift = inverse * gain(2), shift_row(6)
        def go(start, carry, seg=seg, centre=centre, scale=scale, shift=shift):
            at = rows_at(seg.row + start)
            normed = ((res[at, :] - centre) * scale + shift).astype(BF)
            a2[at, :] = normed
            lanes = pl.ds(pl.multiple_of(seg.row + start, BLK) if not isinstance(start, int) else seg.row + start, BLK)
            for part in range(3):
                value = mm(normed, w_qkv[:, part * ch : (part + 1) * ch])
                if part != 1:
                    value = value + shift_row(7 if part == 0 else 8)
                low = value.astype(BF)
                if part:
                    kv[at, part * ch : (part + 1) * ch] = low
                else:
                    low = low * (1.0 / math.sqrt(ch // HEADS))
                qkv_t[part * ch : (part + 1) * ch, lanes] = low.T
            datt_t[:, lanes] = mm(w_proj[...], g[at, :], 1, 1).astype(BF)
            return carry
        each_block(seg, go, 0)

    dkv = r.dkv
    for seg in segs:
        attention(seg, min(512, seg.pixels), kv, qkv_t, datt_t, dkv)

    dqkv = r.dqkv
    r.grad_proj(mm(qkv_t[0:ch, :], g[...]))
    hook("grad_proj")
    zero = jnp.zeros((8, ch), F32)
    sums2 = []
    q_sum, v_sum, g_sum = zero, zero, zero
    for seg, (centre, inverse) in zip(segs, stats2):
        live = r.live(seg.index)
        def go(start, carry, seg=seg, centre=centre, inverse=inverse, live=live):
            s0, s1, q_sum, v_sum, g_sum = carry
            at = rows_at(seg.row + start)
            lanes = pl.ds(pl.multiple_of(seg.row + start, BLK) if not isinstance(start, int) else seg.row + start, BLK)
            value = res[at, :]
            made = mm(qkv_t[0:ch, lanes], w_proj[...], 0, 0) + shift_row(9) + value
            out[at, :] = jnp.where(live, made, 0.0).astype(BF)
            g_sum = g_sum + fold(g[at, :].astype(F32))
            dq = datt_t[:, lanes].T
            dqkv[at, 0:ch] = dq
            dqkv[at, ch : 3 * ch] = dkv[at, :].astype(BF)
            q_sum = q_sum + fold(dq.astype(F32))
            v_sum = v_sum + fold(dkv[at, ch : 2 * ch])
            da2 = mm(dqkv[at, :], w_qkv[...], 1, 1)
            wide[at, :] = da2
            normal = (value - centre) * inverse
            return (s0 + fold(da2), s1 + fold(da2 * normal), q_sum, v_sum, g_sum)
        s0, s1, q_sum, v_sum, g_sum = each_block(seg, go, (zero, zero, q_sum, v_sum, g_sum))
        sums2.append((total(s0), total(s1)))
    hook("out")
    r.grad_qkv(mm(a2[...], dqkv[...], 0, 0))
    hook("grad_qkv")
    terms2 = norm_back_terms(segs, sums2, stats2, [gain(2)] * len(segs), groups)
    y1_sum = zero
    for seg, (centre, inverse), (factor, const, slope) in zip(segs, stats2, terms2):
        def go(start, carry, seg=seg, centre=centre, factor=factor, const=const, slope=slope):
            at = rows_at(seg.row + start)
            d_res = g[at, :].astype(F32) + wide[at, :] * factor - const - (res[at, :] - centre) * slope
            res[at, :] = d_res
            store_triple(triple, seg, start, d_res, True)
            return carry + fold(d_res)
        y1_sum = each_block(seg, go, y1_sum)
    gain2 = sums2[0][1] + sums2[1][1]
    shift6 = sums2[0][0] + sums2[1][0]

    hook("dr")

    for n, columns in enumerate(r.columns):
        conv_weight_grad(kept1, triple, segs, r.grad1, columns)
        hook(("grad1", n))
    cross_weight(r.w1, r.crossed)
    sums1 = []
    for seg, (stretch, centre, inverse, scale, shift) in zip(segs, consts1):
        def go(start, carry, seg=seg, centre=centre, inverse=inverse, scale=scale, shift=shift):
            s0, s1 = carry
            at = rows_at(seg.row + start)
            da1 = conv_back_block(triple, r.crossed, seg, start)
            off = y0[at, :] - centre
            z = off * scale + shift
            sig = sigmoid(z)
            dz = da1 * (sig * (1.0 + z * (1.0 - sig)))
            wide[at, :] = dz
            return (s0 + fold(dz), s1 + fold(dz * (off * inverse)))
        s0, s1 = each_block(seg, go, (zero, zero), ticks("back1"))
        sums1.append((total(s0), total(s1)))
    hook("back1")
    stats = [(centre, inverse) for _, centre, inverse, _, _ in consts1]
    terms1 = norm_back_terms(segs, sums1, stats, scales1, groups)
    y0_sum = zero
    for seg, (centre, inverse), (factor, const, slope) in zip(segs, stats, terms1):
        def go(start, carry, seg=seg, centre=centre, factor=factor, const=const, slope=slope):
            at = rows_at(seg.row + start)
            dy0 = wide[at, :] * factor - const - (y0[at, :] - centre) * slope
            store_triple(triple, seg, start, dy0, True)
            return carry + fold(dy0)
        y0_sum = each_block(seg, go, y0_sum)
    dmod, gain1, shift4 = [], 0.0, 0.0
    for (s0, s1), (stretch, *_) in zip(sums1, consts1):
        dmod.append(jnp.concatenate([gain(1) * s1 + shift_row(4) * s0, s0], axis=1))
        gain1 = gain1 + stretch * s1
        shift4 = shift4 + stretch * s0
    dmod = [d.astype(BF).astype(F32) for d in dmod]
    dmod_sum = dmod[0] + dmod[1]
    r.grad_affine(dmod)

    hook("dy0")

    for n, columns in enumerate(r.columns):
        conv_weight_grad(kept0, triple, segs, r.grad0, columns)
        hook(("grad0", n))
    cross_weight(r.w0, r.crossed)
    sums0 = []
    for seg, (centre, inverse) in zip(segs, stats0):
        scale, shift = inverse * gain(0), shift_row(0)
        def go(start, carry, seg=seg, centre=centre, inverse=inverse, scale=scale, shift=shift):
            s0, s1 = carry
            at = rows_at(seg.row + start)
            da0 = conv_back_block(triple, r.crossed, seg, start)
            off = x[at, :].astype(F32) - centre
            z = off * scale + shift
            sig = sigmoid(z)
            dz = da0 * (sig * (1.0 + z * (1.0 - sig)))
            wide[at, :] = dz
            return (s0 + fold(dz), s1 + fold(dz * (off * inverse)))
        s0, s1 = each_block(seg, go, (zero, zero), ticks("back0"))
        sums0.append((total(s0), total(s1)))
    hook("back0")
    terms0 = norm_back_terms(segs, sums0, stats0, [gain(0)] * len(segs), groups)
    r.rows[...] = jnp.concatenate(
        [
            sums0[0][1] + sums0[1][1],
            gain1,
            gain2,
            sums0[0][0] + sums0[1][0],
            total(y0_sum),
            dmod_sum[:, :ch],
            dmod_sum[:, ch:],
            shift4,
            total(y1_sum),
            shift6,
            total(q_sum),
            total(v_sum),
            total(g_sum),
            jnp.zeros((3, ch), F32),
        ],
        axis=0,
    )
    hook("rows")
    hook("grad")
    for seg, (centre, inverse), (factor, const, slope) in zip(segs, stats0, terms0):
        def go(start, carry, seg=seg, centre=centre, factor=factor, const=const, slope=slope):
            at = rows_at(seg.row + start)
            off = x[at, :].astype(F32) - centre
            grad[at, :] = (res[at, :] + wide[at, :] * factor - const - off * slope).astype(BF)
            return carry
        each_block(seg, go, 0)


def block_scratch(sides, ch):
    _, rows, pads = make_segs(sides)
    return dict(
        triple=pltpu.VMEM((pads, 3 * ch), BF),
        kept0=pltpu.VMEM((pads, ch), BF),
        kept1=pltpu.VMEM((pads, ch), BF),
        y0=pltpu.VMEM((rows, ch), F32),
        res=pltpu.VMEM((rows, ch), F32),
        wide=pltpu.VMEM((rows, ch), F32),
        groups=pltpu.VMEM((ch, ch), BF),
        a2=pltpu.VMEM((rows, ch), BF),
        qkv_t=pltpu.VMEM((3 * ch, rows), BF),
        datt_t=pltpu.VMEM((ch, rows), BF),
        dkv=pltpu.VMEM((rows, 2 * ch), F32),
        dqkv=pltpu.VMEM((rows, 3 * ch), BF),
        crossed=pltpu.VMEM((3 * ch, 3 * ch), BF),
    )


MESH = pl.DeviceIdType.MESH
VMEM_LIMIT = 63 * 2**20
FLIPS = ("s", "x", "y", "d", "xs", "ys", "ds")
OTHER = {"x": "y", "y": "x"}
SMALL = ("p", "m", "n", "q")
WEIGHTS = ("w0", "w1", "wqkv", "wproj")


class Net:
    def __init__(self, names, send, recv):
        self.at = {name: i for i, name in enumerate(names)}
        self.send, self.recv, self.sent = send, recv, []

    def copy(self, name, src, dst, peer):
        i = self.at[name]
        return pltpu.make_async_remote_copy(
            src_ref=src,
            dst_ref=dst,
            send_sem=self.send.at[i],
            recv_sem=self.recv.at[i],
            device_id=peer,
            device_id_type=MESH,
        )

    def push(self, name, make):
        self.copy(name, *make()).start()
        self.sent.append((name, make))

    def take(self, name, dst, peer):
        self.copy(name, dst, dst, peer).wait_recv()

    def drain(self):
        for name, make in self.sent:
            self.copy(name, *make()).wait_send()
        self.sent = []


def spans(rows, pieces):
    tiles = rows // 16
    cuts = [16 * (tiles * i // pieces) for i in range(pieces)] + [rows]
    return [(a, b - a) for a, b in zip(cuts, cuts[1:])]


def gather_units(block):
    units = []
    for name in ("w0", "w1"):
        units += [(name, first, count, axis) for (first, count), axis in zip(spans(block[name], 2), "xy")]
    third = block["wqkv"] // 3
    return units + [
        ("wqkv", 0, 2 * third, "x"),
        ("wqkv", 2 * third, third, "y"),
        ("wproj", 0, block["wproj"], "y"),
    ]


def column_spans(ch):
    return [(0, 2 * ch // 3), (2 * ch // 3, ch)]


def reduce_units(block, ch):
    third = block["wqkv"] // 3
    units = [
        ("wqkv", 0, 2 * third, 0, 3 * ch, "x"),
        ("wqkv", 2 * third, third, 0, 3 * ch, "y"),
        ("wproj", 0, block["wproj"], 0, ch, "y"),
    ]
    for name in ("w1", "w0"):
        for (low, high), pieces in zip(column_spans(ch), (4, 2)):
            for (first, count), axis in zip(spans(block[name], pieces), "xyxy"):
                units.append((name, first, count, low, high - low, axis))
    return units


def transfer_names(out_units, in_units):
    names = [(i, t) for i in range(len(out_units)) for t in ("x", "y", "s", "d", "sx", "sy", "sd")]
    names += [(i, t) for i in range(len(in_units)) for t in "abc"]
    names += [(i, t) for i in list(range(len(in_units))) + ["za", "zr"] for t in ("z0", "z1", "z2")]
    return names + [(what, flip) for what in SMALL for flip in FLIPS]


def packed(rows, height):
    count, columns = rows.shape
    pieces = [rows[i : i + 1, j : j + 128] for i in range(count) for j in range(0, columns, 128)]
    return jnp.concatenate(pieces + [jnp.zeros((height - len(pieces), 128), rows.dtype)], axis=0)


def unpacked(values, count, columns):
    per = columns // 128
    return jnp.concatenate(
        [jnp.concatenate([values[i * per + j : i * per + j + 1, :] for j in range(per)], axis=1) for i in range(count)],
        axis=0,
    )


def fused_kernel(sides, block, r):
    segs, _, _ = make_segs(sides)
    ch = r.triple.shape[1] // 3
    wide_rows = 2 * ch
    out_units, in_units = gather_units(block), reduce_units(block, ch)
    me, z = lax.axis_index("shard"), lax.axis_index("rep")
    core, px, py = me % 2, (me // 2) % 2, me // 4
    outer = (z == 0) | (z == 3)
    inner = jnp.logical_not(outer)

    def index(flip):
        fx = 1 - px if ("x" in flip or "d" in flip) else px
        fy = 1 - py if ("y" in flip or "d" in flip) else py
        fc = 1 - core if "s" in flip else core
        return (fy * 2 + fx) * 2 + fc

    at = {flip: index(flip) for flip in FLIPS + ("",)}
    peer = {flip: (at[flip], z) for flip in FLIPS}
    z_in, z_out, z_cross = (me, jnp.where(z < 2, 1, 2)), (me, jnp.where(z < 2, 0, 3)), (me, 3 - z)
    net = Net(transfer_names(out_units, in_units), r.send, r.recv)

    local = []

    def fetch(src, dst):
        copy = pltpu.make_async_copy(src, dst, r.local.at[len(local)])
        copy.start()
        local.append(copy)
        return copy

    got_x = [fetch(src, r.x.at[s.row : s.row + s.pixels, :]) for src, s in zip((r.big_x, r.small_x), segs)]

    barrier = pltpu.get_barrier_semaphore()
    for flip in FLIPS:
        pl.semaphore_signal(barrier, inc=1, device_id=peer[flip], device_id_type=MESH)

    @pl.when(outer)
    def _():
        pl.semaphore_signal(barrier, inc=1, device_id=z_in, device_id_type=MESH)

    @pl.when(inner)
    def _():
        pl.semaphore_signal(barrier, inc=1, device_id=z_out, device_id_type=MESH)
        pl.semaphore_signal(barrier, inc=1, device_id=z_cross, device_id_type=MESH)

    pl.semaphore_wait(barrier, jnp.where(outer, 8, 9))

    gathered = {name: getattr(r, name) for name in WEIGHTS}
    own = dict(w0=r.own_w0, w1=r.own_w1, wqkv=r.own_wqkv, wproj=r.own_wproj)
    mine = {}

    def part(i, flip):
        name, first, count, _ = out_units[i]
        start = pl.multiple_of(at[flip] * block[name] + first, 16)
        return gathered[name].at[pl.ds(start, count), :]

    def out_start(chosen):
        for flip in ("x", "y", "s"):
            for i in chosen:
                name, first, count, _ = out_units[i]
                net.push(
                    (i, flip),
                    lambda i=i, flip=flip, src=own[name].at[first : first + count, :]: (src, part(i, ""), peer[flip]),
                )
        for i in chosen:
            name, first, count, _ = out_units[i]
            mine[i] = fetch(own[name].at[first : first + count, :], part(i, ""))

    def out_pass(chosen):
        for direct in (True, False):
            for i in chosen:
                axis = out_units[i][3]
                if not direct:
                    axis = OTHER[axis]
                net.take((i, axis), part(i, axis), peer[axis])
                if direct:
                    net.push((i, "d"), lambda i=i, axis=axis: (part(i, axis), part(i, axis), peer[OTHER[axis]]))
                net.push((i, "s" + axis), lambda i=i, axis=axis: (part(i, axis), part(i, axis), peer["s"]))

    def out_late(chosen):
        for i in chosen:
            net.take((i, "d"), part(i, "d"), peer[OTHER[out_units[i][3]]])
            net.push((i, "sd"), lambda i=i: (part(i, "d"), part(i, "d"), peer["s"]))

    def out_end(chosen):
        for i in chosen:
            mine[i].wait()
            for name, flip in (("s", "s"), ("sx", "xs"), ("sy", "ys"), ("sd", "ds")):
                net.take((i, name), part(i, flip), peer["s"])

    grads = dict(w0=r.grad_w0, w1=r.grad_w1, wqkv=r.grad_wqkv, wproj=r.grad_wproj)
    results = dict(w0=r.out_w0, w1=r.out_w1, wqkv=r.out_wqkv, wproj=r.out_wproj)
    done = []

    def unit_ref(i):
        name, first, count, low, width, _ = in_units[i]
        return grads[name], (slice(first, first + count), slice(low, low + width))

    def in_core(chosen):
        for i in chosen:
            ref, span = unit_ref(i)
            net.push((i, "a"), lambda i=i, ref=ref, span=span: (ref.at[(1 - core, slice(None), slice(None)) + span], r.ra[i], peer["s"]))

    def away(i):
        axis = in_units[i][5]
        return (slice(None), 1 - px) if axis == "x" else (1 - py, slice(None))

    def near(i):
        axis = in_units[i][5]
        return (slice(None), px) if axis == "x" else (py, slice(None))

    def cross(i):
        return (1 - py, px) if in_units[i][5] == "x" else (py, 1 - px)

    def add_to(ref, where, value):
        ref[where] = ref[where] + value

    def in_first(chosen):
        for i in chosen:
            ref, span = unit_ref(i)
            axis = in_units[i][5]
            net.take((i, "a"), r.ra[i], peer["s"])
            add_to(ref, (core, slice(None), slice(None)) + span, r.ra[i][...])
            net.push((i, "b"), lambda i=i, ref=ref, span=span, axis=axis: (ref.at[(core,) + away(i) + span], r.rb[i], peer[axis]))

    def in_second(chosen):
        for i in chosen:
            ref, span = unit_ref(i)
            axis = in_units[i][5]
            net.take((i, "b"), r.rb[i], peer[axis])
            add_to(ref, (core,) + near(i) + span, r.rb[i][...])
            net.push((i, "c"), lambda i=i, ref=ref, span=span, axis=axis: (ref.at[(core,) + cross(i) + span], r.rc[i], peer[OTHER[axis]]))

    def z_out_of(i):
        if i == "za":
            return r.own_affine, r.rza
        if i == "zr":
            return r.own_rows, r.rzr
        ref, span = unit_ref(i)
        return ref.at[(core, py, px) + span], r.rz[i]

    def in_third(chosen):
        for i in chosen:
            ref, span = unit_ref(i)
            net.take((i, "c"), r.rc[i], peer[OTHER[in_units[i][5]]])
            add_to(ref, (core, py, px) + span, r.rc[i][...])
            z_first([i])

    def z_first(chosen):
        for i in chosen:
            src, slots = z_out_of(i)

            @pl.when(outer)
            def _():
                net.copy((i, "z0"), src, slots.at[0], z_in).start()

    def z_second(chosen):
        for i in chosen:
            src, slots = z_out_of(i)

            @pl.when(inner)
            def _():
                net.take((i, "z0"), slots.at[0], z_out)
                src[...] = src[...] + slots[0]
                net.copy((i, "z1"), src, slots.at[1], z_cross).start()

    def z_third(chosen):
        for i in chosen:
            src, slots = z_out_of(i)

            @pl.when(inner)
            def _():
                net.take((i, "z1"), slots.at[1], z_cross)
                slots[0] = src[...] + slots[1]
                net.copy((i, "z2"), slots.at[0], slots.at[0], z_out).start()

    def z_end(chosen):
        for i in chosen:
            src, slots = z_out_of(i)

            @pl.when(outer)
            def _():
                net.take((i, "z2"), slots.at[0], z_in)

            if i == "za":
                target = r.out_affine
            elif i == "zr":
                target = r.out_rows
            else:
                name, first, count, low, width, _ = in_units[i]
                target = results[name].at[first : first + count, low : low + width]
            done.append(fetch(slots.at[0], target))

    def z_drain(chosen):
        for i in chosen:
            src, slots = z_out_of(i)

            @pl.when(outer)
            def _():
                net.copy((i, "z0"), src, slots.at[0], z_in).wait_send()

            @pl.when(inner)
            def _():
                net.copy((i, "z1"), src, slots.at[1], z_cross).wait_send()
                net.copy((i, "z2"), slots.at[0], slots.at[0], z_out).wait_send()

    def keep(ref, rows_per):
        def store(row, col, value):
            height, width = value.shape
            start = row
            while start < row + height:
                owner = start // rows_per
                stop = min(row + height, (owner + 1) * rows_per)
                ref[owner % 2, owner // 4, (owner // 2) % 2, start - owner * rows_per : stop - owner * rows_per, col : col + width] = value[
                    start - row : stop - row, :
                ].astype(BF)
                start = stop

        return store

    P0, P1 = [0, 1, 2], [3, 4, 5, 6]
    P2, Q1, Q2 = [7, 8], [9, 10, 11, 12], [13, 14]
    W0, W1, REST = [0, 1], [2, 3], [4, 5, 6]
    copied_out = []
    r.grad = r.out
    r.columns = column_spans(ch)
    r.live = lambda i: r.loads[0, i] > 0
    r.grad0, r.grad1 = keep(r.grad_w0, block["w0"]), keep(r.grad_w1, block["w1"])
    keep_qkv, keep_proj = keep(r.grad_wqkv, block["wqkv"]), keep(r.grad_wproj, block["wproj"])
    r.grad_qkv = lambda value: keep_qkv(0, 0, value)
    r.grad_proj = lambda value: keep_proj(0, 0, value)

    def exchange(what, src, slots):
        each = len(src.shape) == len(slots.shape)
        for flip in FLIPS:
            net.push(
                (what, flip),
                lambda flip=flip: (src.at[at[flip]] if each else src, slots.at[me], peer[flip]),
            )

    def exchanged(what, slots):
        for flip in FLIPS:
            net.take((what, flip), slots.at[at[flip]], peer[flip])

    def hook(name):
        if name == "shifts":
            copied_message.wait()
            exchanged("p", r.messages)
            own_width = 128
            per = ch // 8
            lane = lax.broadcasted_iota(jnp.int32, (8 * own_width, ch), 1)
            sub = lax.broadcasted_iota(jnp.int32, (8 * own_width, ch), 0)
            place = jnp.where(sub % own_width < per, (sub // own_width) * per + sub % own_width, -1)
            spread = jnp.where(lane == place, 1.0, 0.0).astype(BF)
            side_by_side = jnp.concatenate([r.messages[o, 0:16, :] for o in range(8)], axis=1)
            r.params[...] = mm(side_by_side, spread)
            everyone = r.messages[:, 16:32, :].astype(F32).reshape(16, 8, 128)
            chosen = lax.broadcasted_iota(jnp.int32, (16, 8, 128), 1) == me
            r.embeds[...] = jnp.sum(jnp.where(chosen, everyone, 0.0), axis=1).astype(BF)
            copied_affine.wait()
            partial = mm(r.embeds[...], r.waff[...])
            for o in range(8):
                r.mod_out[o] = packed(partial[2 * o : 2 * o + 2, :], 16)
            exchange("m", r.mod_out, r.mod_in)
            r.mod_in[pl.ds(me, 1)] = r.mod_out[pl.ds(me, 1)]
        if name == "w0":
            out_pass(W0)
            out_late(W0)
            out_start(W1)
            out_end(W0)
        if name == "conv0":
            out_pass(W1)
            out_start(REST)
        if name == "affine":
            exchanged("m", r.mod_in)
            r.mod[...] = unpacked(jnp.sum(r.mod_in[...], axis=0), 2, wide_rows)
        if name == "w1":
            out_late(W1)
            out_end(W1)
        if name == "wqkv":
            out_pass(REST)
            out_late(REST)
            out_end(REST)
            for copy in got_g:
                copy.wait()
            for seg in segs:
                rows = slice(seg.row, seg.row + seg.pixels)
                r.g[rows, :] = jnp.where(r.live(seg.index), r.g[rows, :], 0).astype(BF)
        if name == "out":
            for seg, out in zip(segs, (r.big_out, r.small_out)):
                copied_out.append(fetch(r.out.at[seg.row : seg.row + seg.pixels, :], out))
        if name == "grad_qkv":
            in_core(P0)
        if name == "dr":
            in_first(P0)
        if name == ("grad1", 0):
            in_core(P1)
        if name == ("grad1", 1):
            in_core(P2)
            in_second(P0)
            in_first(P1)
        if name == "back1":
            in_second(P1[:2])
            z_second(P0)
        if name == "dy0":
            in_second(P1[2:])
            exchanged("n", r.dmod_in)
            terms = unpacked_rows(r.dmod_in)
            grad = mm(r.embeds[...], terms, 0, 0)
            r.own_affine[...] = grad[0 : block["waff"], :].astype(BF)
            z_first(["za"])
            z_third(P0)
        if name == ("grad0", 0):
            in_core(Q1)
            in_second(P2)
            in_third(P1)
        if name == ("grad0", 1):
            in_core(Q2)
            in_third(P2)
            in_first(Q1)
            z_end(P0)
        if name == "back0":
            in_second(Q1[2:])
            in_second(Q2)
            z_third(P2 + ["za"])
        if name == "rows":
            exchange("q", r.rows, r.rows_in)
            r.rows_in[pl.ds(me, 1)] = r.rows[...][None]
        if name == "grad":
            for copy in copied_out:
                copy.wait()

    def unpacked_rows(ref):
        values = ref[...].astype(F32)
        return jnp.concatenate([unpacked(values[o], 2, wide_rows) for o in range(8)], axis=0).astype(BF)

    def ticks(name):
        if name == "back1":
            return {
                (0, 1): lambda: in_first(P2),
                (0, 2): lambda: in_third(P0),
            }
        if name == "back0":
            return {
                (0, 1): lambda: in_first(Q2),
                (0, 2): lambda: z_second(P1),
                (0, 3): lambda: in_second(Q1[:2]),
                (1, 0): lambda: (z_second(P2 + ["za"]), z_third(P1)),
            }
        return {}

    def grad_affine(rows):
        r.dmod[...] = packed(jnp.concatenate(rows, axis=0), 16).astype(BF)
        exchange("n", r.dmod, r.dmod_in)
        r.dmod_in[pl.ds(me, 1)] = r.dmod[...][None]

    r.grad_affine = grad_affine
    exchange("p", r.message, r.messages)
    copied_message = fetch(r.message, r.messages.at[me])
    out_start(W0)
    r.waff[...] = jnp.zeros_like(r.waff)
    copied_affine = fetch(r.own_waff, r.waff.at[0 : block["waff"], :])
    got_g = [fetch(src, r.g.at[s.row : s.row + s.pixels, :]) for src, s in zip((r.big_g, r.small_g), segs)]
    for copy in got_x:
        copy.wait()
    block_body(sides, r, hook, ticks)

    for seg, out in zip(segs, (r.big_grad, r.small_grad)):
        done.append(fetch(r.grad.at[seg.row : seg.row + seg.pixels, :], out))
    exchanged("q", r.rows_in)
    sums = jnp.concatenate(three_parts(jnp.sum(r.rows_in[...], axis=0)), axis=0).astype(BF)
    lane = lax.broadcasted_iota(jnp.int32, (ch, 128), 1)
    sub = lax.broadcasted_iota(jnp.int32, (ch, 128), 0)
    per = ch // 8
    cut = mm(sums, jnp.where((sub - per * me == lane) & (lane < per), 1.0, 0.0).astype(BF))
    r.own_rows[...] = cut[0:16] + cut[16:32] + cut[32:48]
    z_first(["zr"])
    in_third(Q1[:2])
    z_end(P1 + P2 + ["za"])
    in_third(Q1[2:])
    z_second(["zr"] + Q1[:2])
    in_third(Q2)
    z_second(Q1[2:])
    z_third(["zr"] + Q1[:2])
    z_second(Q2)
    z_third(Q1[2:] + Q2)
    z_end(["zr"] + Q1 + Q2)
    z_drain(P0 + P1 + P2 + Q1 + Q2 + ["za", "zr"])
    net.drain()
    for copy in done:
        copy.wait()


def embed_rows(class_table, sigma_table, labels, sigmas):
    summed = class_table[labels].astype(F32) + sigma_table[sigmas].astype(F32)
    return jax.nn.silu(summed).astype(BF)


def named(names, refs):
    return dict(zip(names, refs))


def fused_call(sides, ch, arrays):
    block = dict(
        w0=arrays["own_w0"].shape[0],
        w1=arrays["own_w1"].shape[0],
        waff=arrays["own_waff"].shape[0],
        wqkv=arrays["own_wqkv"].shape[0],
        wproj=arrays["own_wproj"].shape[0],
    )
    segs, rows, _ = make_segs(sides)
    out_units, in_units = gather_units(block), reduce_units(block, ch)
    width = dict(w0=ch, w1=ch, wqkv=3 * ch, wproj=ch)
    buffer = lambda *shape: pltpu.VMEM(shape, BF)
    wide_buffer = lambda *shape: pltpu.VMEM(shape, F32)
    whole = {name: buffer(8 * block[name], width[name]) for name in WEIGHTS}
    grads = {name: buffer(2, 2, 2, block[name], width[name]) for name in WEIGHTS}
    copies = len(transfer_names(out_units, in_units))
    scratch = dict(
        block_scratch(sides, ch),
        **whole,
        grad_w0=grads["w0"],
        grad_w1=grads["w1"],
        grad_wqkv=grads["wqkv"],
        grad_wproj=grads["wproj"],
        x=buffer(rows, ch),
        g=buffer(rows, ch),
        out=buffer(rows, ch),
        params=wide_buffer(16, ch),
        messages=buffer(8, 32, 128),
        embeds=buffer(16, 128),
        waff=buffer(128, 2 * ch),
        mod_out=wide_buffer(8, 16, 128),
        mod_in=wide_buffer(8, 16, 128),
        mod=wide_buffer(2, 2 * ch),
        dmod=buffer(16, 128),
        dmod_in=buffer(8, 16, 128),
        own_affine=buffer(block["waff"], 2 * ch),
        rza=buffer(2, block["waff"], 2 * ch),
        rows=wide_buffer(16, ch),
        rows_in=wide_buffer(8, 16, ch),
        own_rows=wide_buffer(16, 128),
        rzr=wide_buffer(2, 16, 128),
        send=pltpu.SemaphoreType.DMA((copies,)),
        recv=pltpu.SemaphoreType.DMA((copies,)),
        local=pltpu.SemaphoreType.DMA((48,)),
    )
    slots = [
        [buffer(2, 2, n, w) for _, _, n, _, w, _ in in_units],
        [buffer(2, n, w) for _, _, n, _, w, _ in in_units],
        [buffer(n, w) for _, _, n, _, w, _ in in_units],
        [buffer(2, n, w) for _, _, n, _, w, _ in in_units],
    ]
    big, small = segs[0].pixels, segs[1].pixels
    outs = dict(
        big_out=((big, ch), BF),
        small_out=((small, ch), BF),
        big_grad=((big, ch), BF),
        small_grad=((small, ch), BF),
        out_rows=((16, 128), F32),
        out_affine=((block["waff"], 2 * ch), BF),
        out_w0=((block["w0"], ch), BF),
        out_w1=((block["w1"], ch), BF),
        out_wqkv=((block["wqkv"], 3 * ch), BF),
        out_wproj=((block["wproj"], ch), BF),
    )
    names = list(arrays) + list(outs) + list(scratch)

    def kernel(*refs):
        r = types.SimpleNamespace(**dict(zip(names, refs)))
        rest = list(refs[len(names) :])
        n = len(in_units)
        r.ra, r.rb, r.rc, r.rz = rest[:n], rest[n : 2 * n], rest[2 * n : 3 * n], rest[3 * n :]
        fused_kernel(sides, block, r)

    results = pl.pallas_call(
        kernel,
        out_shape=[jax.ShapeDtypeStruct(*shape) for shape in outs.values()],
        in_specs=[pl.BlockSpec(memory_space=pltpu.SMEM)] + [pl.BlockSpec(memory_space=pl.ANY)] * (len(arrays) - 1),
        out_specs=[pl.BlockSpec(memory_space=pl.ANY)] * len(outs),
        scratch_shapes=list(scratch.values()) + sum(slots, []),
        compiler_params=pltpu.CompilerParams(
            collective_id=0, has_side_effects=True, vmem_limit_bytes=VMEM_LIMIT
        ),
    )(*arrays.values())
    return results


def finish_call(results, per):
    images, rows, weights = results[:4], results[4], results[5:]
    outs = [jax.ShapeDtypeStruct(image.shape, image.dtype) for image in images]
    outs += [jax.ShapeDtypeStruct((3, per), F32), jax.ShapeDtypeStruct((10, per), F32)]
    outs += [jax.ShapeDtypeStruct(weight.shape, F32) for weight in weights]
    total_in, total_out = len(results), len(outs)

    def kernel(*refs):
        sources, targets = refs[:total_in], refs[total_in : total_in + total_out]
        rest = refs[total_in + total_out :]
        held, made, sems = rest[:total_in], rest[total_in:-1], rest[-1]
        inward = [pltpu.make_async_copy(s, h, sems.at[i]) for i, (s, h) in enumerate(zip(sources, held))]
        for copy in inward:
            copy.start()
        outward = []

        def send(source, target):
            copy = pltpu.make_async_copy(source, target, sems.at[total_in + len(outward)])
            copy.start()
            outward.append(copy)

        for i in range(5, total_in):
            inward[i].wait()
            made[i - 3][...] = held[i][...].astype(F32)
            send(made[i - 3], targets[i + 1])
        for i in range(4):
            inward[i].wait()
            send(held[i], targets[i])
        inward[4].wait()
        made[0][...] = held[4][0:3, 0:per]
        made[1][...] = held[4][3:13, 0:per]
        send(made[0], targets[4])
        send(made[1], targets[5])
        for copy in outward:
            copy.wait()

    any_spec = pl.BlockSpec(memory_space=pl.ANY)
    return pl.pallas_call(
        kernel,
        out_shape=outs,
        in_specs=[any_spec] * total_in,
        out_specs=[any_spec] * total_out,
        scratch_shapes=[pltpu.VMEM(array.shape, array.dtype) for array in results]
        + [pltpu.VMEM(out.shape, out.dtype) for out in outs[4:]]
        + [pltpu.SemaphoreType.DMA((total_in + total_out,))],
        compiler_params=pltpu.CompilerParams(vmem_limit_bytes=VMEM_LIMIT),
    )(*results)


def plain_call(sides, ch, arrays):
    _, rows, _ = make_segs(sides)
    scratch = dict(
        block_scratch(sides, ch), mod=pltpu.VMEM((16, 2 * ch), F32), masked=pltpu.VMEM((rows, ch), BF)
    )
    outs = dict(
        out=((rows, ch), BF),
        grad=((rows, ch), BF),
        terms0=((9 * ch, ch), BF),
        terms1=((9 * ch, ch), BF),
        affine=((2 * ch, 2 * ch), BF),
        terms_qkv=((ch, 3 * ch), BF),
        terms_proj=((ch, ch), BF),
        rows=((16, ch), F32),
    )
    names = list(arrays) + list(outs) + list(scratch)

    def kernel(*refs):
        r = types.SimpleNamespace(**dict(zip(names, refs)))
        segs, _, _ = make_segs(sides)
        given = r.g
        r.live = lambda i: r.loads[0, i] > 0
        r.g = r.masked
        r.columns = [(0, ch)]
        for seg in segs:
            span = slice(seg.row, seg.row + seg.pixels)
            r.masked[span, :] = jnp.where(r.live(seg.index), given[span, :], 0).astype(BF)

        def hook(name):
            if name == "affine":
                r.mod[...] = mm(r.emb[...], r.waff[...])

        def keep(ref):
            def store(row, col, value):
                ref[row : row + value.shape[0], col : col + value.shape[1]] = value.astype(BF)

            return store

        def grad_affine(terms):
            zeros = jnp.zeros((14, 2 * ch), F32)
            r.affine[...] = mm(r.emb[...], jnp.concatenate(terms + [zeros], axis=0).astype(BF), 0, 0).astype(BF)

        r.grad0, r.grad1 = keep(r.terms0), keep(r.terms1)
        r.grad_qkv = lambda value: keep(r.terms_qkv)(0, 0, value)
        r.grad_proj = lambda value: keep(r.terms_proj)(0, 0, value)
        r.grad_affine = grad_affine
        block_body(sides, r, hook)

    return pl.pallas_call(
        kernel,
        out_shape=[jax.ShapeDtypeStruct(*shape) for shape in outs.values()],
        in_specs=[pl.BlockSpec(memory_space=pltpu.SMEM)]
        + [pl.BlockSpec(memory_space=pltpu.VMEM)] * (len(arrays) - 1),
        out_specs=[pl.BlockSpec(memory_space=pltpu.VMEM)] * len(outs),
        scratch_shapes=list(scratch.values()),
        compiler_params=pltpu.CompilerParams(vmem_limit_bytes=VMEM_LIMIT),
    )(*arrays.values())


def on_device(
    fused,
    big_images,
    small_images,
    big_labels,
    small_labels,
    big_sigmas,
    small_sigmas,
    loads,
    class_table,
    sigma_table,
    norm_gains,
    biases,
    w_conv0,
    w_conv1,
    w_affine,
    w_qkv,
    w_proj,
    big_cotangent,
    small_cotangent,
):
    sides = (big_images.shape[1], small_images.shape[1])
    ch = big_images.shape[-1]
    flat = lambda array: array.reshape(-1, ch)
    big_embed = embed_rows(class_table, sigma_table, big_labels, big_sigmas)
    small_embed = embed_rows(class_table, sigma_table, small_labels, small_sigmas)
    emb = jnp.concatenate([big_embed, small_embed], axis=0)
    own_rows = jnp.concatenate([norm_gains, biases], axis=0)
    shapes = [big_images.shape, small_images.shape] * 2
    if fused:
        per = own_rows.shape[1]
        slices = emb.reshape(16, -1)
        message = jnp.concatenate(
            [
                jnp.pad(own_rows, ((0, 3), (0, 128 - per))),
                jnp.pad(slices, ((0, 0), (0, 128 - slices.shape[1]))),
            ],
            axis=0,
        )
        made = fused_call(
            sides,
            ch,
            dict(
                loads=loads,
                big_x=flat(big_images),
                small_x=flat(small_images),
                big_g=flat(big_cotangent),
                small_g=flat(small_cotangent),
                message=message,
                own_w0=w_conv0,
                own_w1=w_conv1,
                own_waff=w_affine,
                own_wqkv=w_qkv,
                own_wproj=w_proj,
            ),
        )
        made = finish_call(made, per)
        images, gains, shifts = made[:4], made[4], made[5]
        affine, first, second, qkv, proj = made[6:]
        weights = [first, second, affine, qkv, proj]
    else:
        gather = lambda array, axis=0: lax.all_gather(array, "shard", axis=axis, tiled=True)
        out, grad, terms0, terms1, affine, terms_qkv, terms_proj, rows = plain_call(
            sides,
            ch,
            dict(
                loads=loads,
                x=jnp.concatenate([flat(big_images), flat(small_images)], axis=0),
                g=jnp.concatenate([flat(big_cotangent), flat(small_cotangent)], axis=0),
                emb=jnp.pad(emb, ((0, 14), (0, 0))),
                params=jnp.pad(gather(own_rows, 1).astype(F32), ((0, 3), (0, 0))),
                w0=gather(w_conv0),
                w1=gather(w_conv1),
                waff=gather(w_affine),
                wqkv=gather(w_qkv),
                wproj=gather(w_proj),
            ),
        )

        def owned(terms, axis=0):
            mine = lax.psum_scatter(terms, "shard", scatter_dimension=axis, tiled=True)
            return lax.psum(mine, "rep").astype(F32)

        big = sides[0] * sides[0]
        images = [out[:big], out[big:], grad[:big], grad[big:]]
        sums = owned(rows, 1)
        gains, shifts = sums[:3], sums[3:13]
        weights = [owned(terms) for terms in (terms0, terms1, affine, terms_qkv, terms_proj)]
    return tuple(image.reshape(shape) for image, shape in zip(images, shapes)) + (gains, shifts, *weights)


def solution(mesh):
    fused = mesh.shape["shard"] == 8 and mesh.shape["rep"] == 4
    split = P(("shard", "rep"))
    image = P(("shard", "rep"), None, None, None)
    rows, columns = P("shard", None), P(None, "shard")
    return jax.shard_map(
        lambda *arrays: on_device(fused, *arrays),
        mesh=mesh,
        in_specs=(image, image, split, split, split, split, P(("shard", "rep"), None), P(), P(), columns, columns)
        + (rows,) * 5
        + (image, image),
        out_specs=(image,) * 4 + (columns,) * 2 + (rows,) * 5,
        check_vma=False,
    )
```

time: 939 us -> 155 us (0.17); the launches traced: 928 us -> 155 us
  waiting for transfers between devices: 362 us -> 0 us
  local copies, waits for them, and re-layouts: 202 us -> 0.09 us
  Pallas kernels: 0 us -> 149 us
  matrix products: 148 us -> 0 us
  other arithmetic: 128 us -> 2.13 us
  blocking collectives: 63.3 us -> 0 us
  between operations: 19.5 us -> 3.44 us
    reduce_scatter x5 -> x0, waiting for transfers between devices: 258 us -> none  [the longest x1 87.8 us: on_device(): lax.psum_scatter(grad_qkv.astype(jnp.bfloat16), 'shard', scatter_dimensio...]
    pallas_call x0 -> x2, Pallas kernels: none -> 149 us  [the longest x1 145 us: fused_call(): pl.pallas_call(kernel, out_shape=[jax.ShapeDtypeStruct(*shape) for shape...]
    dot_general x47 -> x0, matrix products: 148 us -> none  [the longest x8 32.5 us: contract_rows(): lax.dot_general(left_side, right_side, (((0,), (0,)), ((), ())), preferre...]
    unnamed x13 -> x0, waiting for transfers between devices: 73.5 us -> none
    reduce_sum x71 -> x0, other arithmetic: 53.7 us -> none  [the longest x31 20.2 us: group_norm(): spread = jnp.mean(jnp.square(grouped - centre), axis=(0, 2), keepdims=True)]
    unnamed x414 -> x0, local copies, waits for them, and re-layouts: 51.7 us -> none
    convert_element_type x32 -> x1, other arithmetic: 45.6 us -> 0.81 us  [embed_rows(): return jax.nn.silu(summed).astype(BF)]
    all_gather x4 -> x0, blocking collectives: 42.3 us -> none  [the longest x1 14.3 us: on_device(): lax.all_gather(w_qkv, 'shard', axis=0, tiled=True)]
  transfers between devices with their start and end apart: 11 -> 0, of which waited for: 8 -> 0; matrix products, arithmetic and copies ran while one was open for 6% -> 0% of each run, Pallas kernels for 0% -> 0%
where the time goes in v1:
time: 155 us
  Pallas kernels  149 us (96%)
  between operations  3.44 us (2%)
  other arithmetic  2.13 us (1%)
    pallas_call x1, Pallas kernels, fused_call(): pl.pallas_call(kernel, out_shape=[jax.ShapeDtypeStruct(*shape) for shape...  145 us
    pallas_call x1, Pallas kernels, finish_call(): pl.pallas_call(kernel, out_shape=outs, in_specs=[any_spec] * total_in, ou...  3.66 us

profile of v1, /device:TPU:0, one launch (start us, length us, event | category | flops | bytes accessed | tf_op | source)
XLA Modules:
  0.0 154.7 jit_solution(692385405240327909)
XLA Ops:
  3.2 0.7 fusion.7
  4.0 0.8 fusion.11
  4.8 0.1 reshape.141
  4.9 0.6 fusion.1.refs_5_
  5.5 145.4 %shard_map.257 = (bf16[1024,384]{1,0:T(8,128)(2,1)}, bf16[256,384]{1,0:T(8,128)(2,1)}, bf16[1024,384]{1,0:T(8,128)(2,1)}, bf16[256,384]{1,0:T(8,128)(2,1)}, f32[...) custom-call(s32[1,2]{1,0:T(1,128)} %refs_0_.1, ...), custom_call_target="tpu_custom_call" | custom-call | tf_op jit(solution)/shard_map/pallas_call | solution.py:1085
  150.9 3.7 %shard_map.258 = (bf16[1024,384]{1,0:T(8,128)(2,1)}, bf16[256,384]{1,0:T(8,128)(2,1)}, bf16[1024,384]{1,0:T(8,128)(2,1)}, bf16[256,384]{1,0:T(8,128)(2,1)}, f32[...) custom-call(bf16[1024,384]{1,0:T(8,128)(2,1)} %get-tuple-element.32., ...), custom_call_target="tpu_custom_call" | custom-call | tf_op jit(solution)/shard_map/pallas_call | solution.py:1135
  (1 shorter events, 0.0 us)

commit v2 on v1

--- a/solution.py
+++ b/solution.py
@@ -58,7 +58,11 @@
 
     def step(i, c):
         for n, act in due.items():
-            pl.when(i == n)(act)
+
+            @pl.when(i == n)
+            def _(act=act):
+                act()
+
         return body(pl.multiple_of(i * BLK, BLK), c)
 
     return lax.fori_loop(0, count, step, carry)
@@ -182,11 +186,12 @@
     lax.fori_loop(0, 3, step, 0)
 
 
-def conv_weight_grad(kept, triple, segs, store, columns):
+def conv_weight_grad(kept, triple, segs, store, columns, ticks):
     channels = kept.shape[1]
     first_col, last_col = columns
     width = last_col - first_col
     for a in range(3):
+        ticks.get(a, lambda: None)()
         out = None
         for seg in segs:
             first = seg.pad + (a - 1) * seg.side
@@ -203,61 +208,93 @@
             store((3 * a + b) * channels, first_col, out[:, b * width : (b + 1) * width])
 
 
-def attention(seg, block, keyvalue, qkv_t, datt_t, dkv):
-    channels = datt_t.shape[0]
-    head = channels // HEADS
-    pair = 2 * head
-    pixels = seg.pixels
-    span = pl.ds(seg.row, pixels)
-    place = lax.broadcasted_iota(jnp.int32, (pair, 1), 0)
+class HeadPart:
+    def __init__(self, refs, span, chunk, pair_row, half, at):
+        self.qkv_t, self.datt_t, self.keyvalue, self.dkv = refs
+        self.first, self.pixels, self.chunk = span.start, span.stop - span.start, chunk
+        self.channels = self.datt_t.shape[0]
+        self.head = self.channels // HEADS
+        self.pair, self.half, self.at = pair_row, half, at
+        self.row = pair_row + half * self.head
+        self.scores, self.probs, self.d_scores = {}, {}, {}
+        self.peak, self.sums, self.out, self.dq = None, 0.0, 0.0, 0.0
+
+    def keys(self, n):
+        return slice(self.first + n * self.chunk, self.first + (n + 1) * self.chunk)
+
+    def last(self, n):
+        return n == self.pixels // self.chunk - 1
+
+    def score(self, n):
+        width = 2 * self.head
+        rows = pl.ds(self.pair, width)
+        if n == 0:
+            place = lax.broadcasted_iota(jnp.int32, (width, 1), 0)
+            mine = (place < self.head) if self.half == 0 else (place >= self.head)
+            self.q = jnp.where(mine, self.qkv_t[rows, self.at], 0).astype(BF)
+            self.d_att = jnp.where(mine, self.datt_t[rows, self.at], 0).astype(F32)
+        self.scores[n] = mm(self.keyvalue[self.keys(n), pl.ds(self.channels + self.pair, width)], self.q)
+        peak = jnp.max(self.scores[n], axis=0, keepdims=True)
+        self.peak = peak if self.peak is None else jnp.maximum(self.peak, peak)
+
+    def attend(self, n):
+        probs = jnp.exp(self.scores.pop(n) - self.peak)
+        self.sums = self.sums + jnp.sum(probs, axis=0, keepdims=True)
+        self.probs[n] = probs.astype(BF)
+        values_t = self.qkv_t[pl.ds(2 * self.channels + self.row, self.head), self.keys(n)]
+        self.out = self.out + mm(values_t, self.probs[n])
+        if self.last(n):
+            inverse = 1.0 / self.sums
+            out = self.out * inverse
+            self.d_att = (self.d_att * inverse).astype(BF)
+            mine = self.d_att[self.half * self.head : (self.half + 1) * self.head].astype(F32)
+            self.dots = jnp.sum(mine * out, axis=0, keepdims=True)
+            self.qkv_t[pl.ds(self.row, self.head), self.at] = out.astype(BF)
+
+    def back(self, n):
+        width = 2 * self.head
+        lanes = pl.ds(self.channels + self.pair, width)
+        d_probs = mm(self.keyvalue[self.keys(n), pl.ds(2 * self.channels + self.pair, width)], self.d_att)
+        self.d_scores[n] = (self.probs[n].astype(F32) * (d_probs - self.dots)).astype(BF)
+        self.dkv[self.keys(n), lanes] += mm(self.probs.pop(n), self.d_att, 1, 1)
+
+    def last_products(self, n):
+        d_scores = self.d_scores.pop(n)
+        self.dkv[self.keys(n), pl.ds(self.pair, 2 * self.head)] += mm(d_scores, self.q, 1, 1)
+        keys_t = self.qkv_t[pl.ds(self.channels + self.row, self.head), self.keys(n)]
+        self.dq = self.dq + mm(keys_t, d_scores)
+        if self.last(n):
+            self.datt_t[pl.ds(self.row, self.head), self.at] = (self.dq * (1.0 / math.sqrt(self.head))).astype(BF)
+
+
+def attention(seg, block, chunk, keyvalue, qkv_t, datt_t, dkv):
+    pair = 2 * datt_t.shape[0] // HEADS
+    span = slice(seg.row, seg.row + seg.pixels)
+    dkv[span, :] = jnp.zeros((seg.pixels, dkv.shape[1]), F32)
 
     def heads(index, carry):
-        ro = pl.multiple_of(index * pair, pair)
-        keys = keyvalue[span, pl.ds(channels + ro, pair)]
-        values = keyvalue[span, pl.ds(2 * channels + ro, pair)]
-
-        def queries(step, inner):
-            r = seg.row + step * block
-            at = pl.ds(pl.multiple_of(r, block) if not isinstance(r, int) else r, block)
-            q_pair = qkv_t[pl.ds(ro, pair), at]
-            d_pair = datt_t[pl.ds(ro, pair), at]
-            dk, dv = 0, 0
-            for h in range(2):
-                mine = (place < head) if h == 0 else (place >= head)
-                q = jnp.where(mine, q_pair, 0).astype(BF)
-                scores = mm(keys, q)
-                peak = jnp.max(scores, axis=0, keepdims=True)
-                probs = jnp.exp(scores - peak)
-                inverse = 1.0 / jnp.sum(probs, axis=0, keepdims=True)
-                probs_b = probs.astype(BF)
-                k_t = qkv_t[pl.ds(channels + ro + h * head, head), span]
-                v_t = qkv_t[pl.ds(2 * channels + ro + h * head, head), span]
-                out_t = mm(v_t, probs_b) * inverse
-                d_att = (jnp.where(mine, d_pair, 0).astype(F32) * inverse).astype(BF)
-                dots = jnp.sum(d_att[h * head : (h + 1) * head].astype(F32) * out_t, axis=0, keepdims=True)
-                d_probs = mm(values, d_att)
-                d_scores = (probs * (d_probs - dots)).astype(BF)
-                qkv_t[pl.ds(ro + h * head, head), at] = out_t.astype(BF)
-                datt_t[pl.ds(ro + h * head, head), at] = (mm(k_t, d_scores) * (1.0 / math.sqrt(head))).astype(BF)
-                dk = dk + mm(d_scores, q, 1, 1)
-                dv = dv + mm(probs_b, d_att, 1, 1)
-            if isinstance(step, int):
-                dkv[span, pl.ds(ro, pair)] = dk
-                dkv[span, pl.ds(channels + ro, pair)] = dv
-            else:
-                first = step == 0
-                dkv[span, pl.ds(ro, pair)] = dk + jnp.where(first, 0.0, dkv[span, pl.ds(ro, pair)])
-                dkv[span, pl.ds(channels + ro, pair)] = dv + jnp.where(first, 0.0, dkv[span, pl.ds(channels + ro, pair)])
-            return inner
-
-        if pixels == block:
-            return queries(0, carry)
-        return lax.fori_loop(0, pixels // block, queries, carry)
+        row = pl.multiple_of(index * pair, pair)
+        parts = [
+            HeadPart((qkv_t, datt_t, keyvalue, dkv), span, chunk, row, half, slice(first, first + block))
+            for first in range(span.start, span.stop, block)
+            for half in range(2)
+        ]
+        for k in range(-1, len(parts) + 2):
+            for n in range(seg.pixels // chunk):
+                if 0 <= k - 2 < len(parts):
+                    parts[k - 2].last_products(n)
+                if 0 <= k - 1 < len(parts):
+                    parts[k - 1].back(n)
+                if 0 <= k < len(parts):
+                    parts[k].attend(n)
+                if 0 <= k + 1 < len(parts):
+                    parts[k + 1].score(n)
+        return carry
 
     lax.fori_loop(0, HEADS // 2, heads, 0)
 
 
-def block_body(sides, r, hook=lambda name: None, ticks=lambda name: None):
+def block_body(sides, r, hook=lambda name: None, ticks=lambda name: {}):
     segs, rows_all, pad_all = make_segs(sides)
     ch = r.x.shape[1]
     x, g, out, grad = r.x, r.g, r.out, r.grad
@@ -357,8 +394,9 @@
 
     dkv = r.dkv
     for seg in segs:
-        attention(seg, min(512, seg.pixels), kv, qkv_t, datt_t, dkv)
-
+        attention(seg, min(512, seg.pixels), min(256, seg.pixels), kv, qkv_t, datt_t, dkv)
+
+    hook("att")
     dqkv = r.dqkv
     r.grad_proj(mm(qkv_t[0:ch, :], g[...]))
     hook("grad_proj")
@@ -366,14 +404,10 @@
     sums2 = []
     q_sum, v_sum, g_sum = zero, zero, zero
     for seg, (centre, inverse) in zip(segs, stats2):
-        live = r.live(seg.index)
-        def go(start, carry, seg=seg, centre=centre, inverse=inverse, live=live):
+        def go(start, carry, seg=seg, centre=centre, inverse=inverse):
             s0, s1, q_sum, v_sum, g_sum = carry
             at = rows_at(seg.row + start)
             lanes = pl.ds(pl.multiple_of(seg.row + start, BLK) if not isinstance(start, int) else seg.row + start, BLK)
-            value = res[at, :]
-            made = mm(qkv_t[0:ch, lanes], w_proj[...], 0, 0) + shift_row(9) + value
-            out[at, :] = jnp.where(live, made, 0.0).astype(BF)
             g_sum = g_sum + fold(g[at, :].astype(F32))
             dq = datt_t[:, lanes].T
             dqkv[at, 0:ch] = dq
@@ -382,11 +416,10 @@
             v_sum = v_sum + fold(dkv[at, ch : 2 * ch])
             da2 = mm(dqkv[at, :], w_qkv[...], 1, 1)
             wide[at, :] = da2
-            normal = (value - centre) * inverse
+            normal = (res[at, :] - centre) * inverse
             return (s0 + fold(da2), s1 + fold(da2 * normal), q_sum, v_sum, g_sum)
-        s0, s1, q_sum, v_sum, g_sum = each_block(seg, go, (zero, zero, q_sum, v_sum, g_sum))
+        s0, s1, q_sum, v_sum, g_sum = each_block(seg, go, (zero, zero, q_sum, v_sum, g_sum), ticks("out"))
         sums2.append((total(s0), total(s1)))
-    hook("out")
     r.grad_qkv(mm(a2[...], dqkv[...], 0, 0))
     hook("grad_qkv")
     terms2 = norm_back_terms(segs, sums2, stats2, [gain(2)] * len(segs), groups)
@@ -395,18 +428,17 @@
         def go(start, carry, seg=seg, centre=centre, factor=factor, const=const, slope=slope):
             at = rows_at(seg.row + start)
             d_res = g[at, :].astype(F32) + wide[at, :] * factor - const - (res[at, :] - centre) * slope
-            res[at, :] = d_res
+            dkv[at, 0:ch] = d_res
             store_triple(triple, seg, start, d_res, True)
             return carry + fold(d_res)
-        y1_sum = each_block(seg, go, y1_sum)
+        y1_sum = each_block(seg, go, y1_sum, ticks("dr"))
     gain2 = sums2[0][1] + sums2[1][1]
     shift6 = sums2[0][0] + sums2[1][0]
 
     hook("dr")
 
-    for n, columns in enumerate(r.columns):
-        conv_weight_grad(kept1, triple, segs, r.grad1, columns)
-        hook(("grad1", n))
+    conv_weight_grad(kept1, triple, segs, r.grad1, (0, ch), ticks(("grad1", 0)))
+    hook("grad1")
     cross_weight(r.w1, r.crossed)
     sums1 = []
     for seg, (stretch, centre, inverse, scale, shift) in zip(segs, consts1):
@@ -432,7 +464,7 @@
             dy0 = wide[at, :] * factor - const - (y0[at, :] - centre) * slope
             store_triple(triple, seg, start, dy0, True)
             return carry + fold(dy0)
-        y0_sum = each_block(seg, go, y0_sum)
+        y0_sum = each_block(seg, go, y0_sum, ticks("dy0"))
     dmod, gain1, shift4 = [], 0.0, 0.0
     for (s0, s1), (stretch, *_) in zip(sums1, consts1):
         dmod.append(jnp.concatenate([gain(1) * s1 + shift_row(4) * s0, s0], axis=1))
@@ -445,7 +477,7 @@
     hook("dy0")
 
     for n, columns in enumerate(r.columns):
-        conv_weight_grad(kept0, triple, segs, r.grad0, columns)
+        conv_weight_grad(kept0, triple, segs, r.grad0, columns, ticks(("grad0", n)))
         hook(("grad0", n))
     cross_weight(r.w0, r.crossed)
     sums0 = []
@@ -485,14 +517,23 @@
         axis=0,
     )
     hook("rows")
-    hook("grad")
+    for seg in segs:
+        live = r.live(seg.index)
+        def go(start, carry, seg=seg, live=live):
+            at = rows_at(seg.row + start)
+            lanes = pl.ds(pl.multiple_of(seg.row + start, BLK) if not isinstance(start, int) else seg.row + start, BLK)
+            made = mm(qkv_t[0:ch, lanes], w_proj[...], 0, 0) + shift_row(9) + res[at, :]
+            out[at, :] = jnp.where(live, made, 0.0).astype(BF)
+            return carry
+        each_block(seg, go, 0, ticks("late"))
+    hook("late")
     for seg, (centre, inverse), (factor, const, slope) in zip(segs, stats0, terms0):
         def go(start, carry, seg=seg, centre=centre, factor=factor, const=const, slope=slope):
             at = rows_at(seg.row + start)
             off = x[at, :].astype(F32) - centre
-            grad[at, :] = (res[at, :] + wide[at, :] * factor - const - off * slope).astype(BF)
+            grad[at, :] = (dkv[at, 0:ch] + wide[at, :] * factor - const - off * slope).astype(BF)
             return carry
-        each_block(seg, go, 0)
+        each_block(seg, go, 0, ticks("grad"))
 
 
 def block_scratch(sides, ch):
@@ -522,6 +563,34 @@
 WEIGHTS = ("w0", "w1", "wqkv", "wproj")
 
 
+SCHEDULE = {
+    "grad_qkv": ((0, 0), (1, 0)),
+    ("dr", 0, 2): ((0, 1),),
+    ("dr", 0, 3): ((1, 1),),
+    "grad1": ((0, 2), (1, 2), (2, 0), (3, 0), (4, 0), (5, 0)),
+    ("back1", 0, 1): ((2, 1), (3, 1), (0, 3), (1, 3)),
+    ("back1", 0, 3): ((4, 1), (0, 4), (5, 1)),
+    "back1": ((1, 4), (0, 5), (2, 2), (3, 2)),
+    ("dy0", 1, 0): ((1, 5), (4, 2), (5, 2)),
+    ("grad0", 0, 1): ((2, 3), (3, 3)),
+    ("grad0", 0): ((4, 3), (5, 3), (12, 3), (6, 0), (7, 0), (2, 4), (8, 0), (9, 0)),
+    ("grad0", 1, 1): ((6, 1), (7, 1)),
+    ("grad0", 1, 2): ((3, 4),),
+    ("grad0", 1): ((10, 0), (11, 0), (8, 1), (2, 5), (9, 1)),
+    ("back0", 0, 1): ((4, 4), (3, 5), (6, 2), (7, 2)),
+    ("back0", 0, 2): ((5, 4), (10, 1), (11, 1)),
+    ("back0", 0, 3): ((4, 5), (8, 2), (7, 3), (6, 3), (9, 2), (12, 4)),
+    ("back0", 1, 0): ((5, 5),),
+    "back0": ((7, 4), (10, 2), (11, 2), (6, 4), (9, 3), (8, 3)),
+    ("late", 0, 1): ((12, 5),),
+    ("late", 0, 2): ((10, 3), (7, 5), (9, 4), (11, 3)),
+    ("late", 1, 0): ((6, 5), (8, 4)),
+    ("grad", 0, 0): ((9, 5), (10, 4), (13, 3)),
+    ("grad", 0, 2): ((11, 4), (13, 4), (8, 5)),
+}
+TAIL = ((0, 6), (1, 6), (10, 5), (7, 6), (2, 6), (3, 6), (4, 6), (6, 6), (5, 6), (12, 6), (11, 5), (13, 5), (9, 6), (8, 6), (10, 6), (11, 6), (13, 6))
+
+
 class Net:
     def __init__(self, names, send, recv):
         self.at = {name: i for i, name in enumerate(names)}
@@ -557,40 +626,27 @@
     return [(a, b - a) for a, b in zip(cuts, cuts[1:])]
 
 
-def gather_units(block):
-    units = []
-    for name in ("w0", "w1"):
-        units += [(name, first, count, axis) for (first, count), axis in zip(spans(block[name], 2), "xy")]
-    third = block["wqkv"] // 3
-    return units + [
-        ("wqkv", 0, 2 * third, "x"),
-        ("wqkv", 2 * third, third, "y"),
-        ("wproj", 0, block["wproj"], "y"),
-    ]
-
-
 def column_spans(ch):
     return [(0, 2 * ch // 3), (2 * ch // 3, ch)]
 
 
 def reduce_units(block, ch):
-    third = block["wqkv"] // 3
-    units = [
-        ("wqkv", 0, 2 * third, 0, 3 * ch, "x"),
-        ("wqkv", 2 * third, third, 0, 3 * ch, "y"),
-        ("wproj", 0, block["wproj"], 0, ch, "y"),
-    ]
-    for name in ("w1", "w0"):
-        for (low, high), pieces in zip(column_spans(ch), (4, 2)):
-            for (first, count), axis in zip(spans(block[name], pieces), "xyxy"):
-                units.append((name, first, count, low, high - low, axis))
+    units = [("both", 0, block["wqkv"], 0, 2 * ch, "x"), ("both", 0, block["wqkv"], 2 * ch, 2 * ch, "y")]
+    for (first, count), axis in zip(spans(block["w1"], 4), "xyxy"):
+        units.append(("w1", first, count, 0, ch, axis))
+    for (low, high), pieces in zip(column_spans(ch), (4, 2)):
+        for (first, count), axis in zip(spans(block["w0"], pieces), "xyxy"):
+            units.append(("w0", first, count, low, high - low, axis))
     return units
 
 
-def transfer_names(out_units, in_units):
-    names = [(i, t) for i in range(len(out_units)) for t in ("x", "y", "s", "d", "sx", "sy", "sd")]
+OUT_STEPS = ("x0", "x1", "y0", "y1", "s", "d0", "d1", "zx", "zy", "zd", "sx", "sy", "sd", "ox", "oy", "od")
+
+
+def transfer_names(in_units):
+    names = [(-1 - i, t) for i in range(len(WEIGHTS)) for t in OUT_STEPS]
     names += [(i, t) for i in range(len(in_units)) for t in "abc"]
-    names += [(i, t) for i in list(range(len(in_units))) + ["za", "zr"] for t in ("z0", "z1", "z2")]
+    names += [(i, t) for i in range(len(in_units) + 2) for t in ("z0", "z1", "z2")]
     return names + [(what, flip) for what in SMALL for flip in FLIPS]
 
 
@@ -612,7 +668,7 @@
     segs, _, _ = make_segs(sides)
     ch = r.triple.shape[1] // 3
     wide_rows = 2 * ch
-    out_units, in_units = gather_units(block), reduce_units(block, ch)
+    in_units = reduce_units(block, ch)
     me, z = lax.axis_index("shard"), lax.axis_index("rep")
     core, px, py = me % 2, (me // 2) % 2, me // 4
     outer = (z == 0) | (z == 3)
@@ -627,7 +683,7 @@
     at = {flip: index(flip) for flip in FLIPS + ("",)}
     peer = {flip: (at[flip], z) for flip in FLIPS}
     z_in, z_out, z_cross = (me, jnp.where(z < 2, 1, 2)), (me, jnp.where(z < 2, 0, 3)), (me, 3 - z)
-    net = Net(transfer_names(out_units, in_units), r.send, r.recv)
+    net = Net(transfer_names(in_units), r.send, r.recv)
 
     local = []
 
@@ -654,61 +710,87 @@
 
     pl.semaphore_wait(barrier, jnp.where(outer, 8, 9))
 
-    gathered = {name: getattr(r, name) for name in WEIGHTS}
-    own = dict(w0=r.own_w0, w1=r.own_w1, wqkv=r.own_wqkv, wproj=r.own_wproj)
+    gathered = [getattr(r, name) for name in WEIGHTS]
+    own = (r.own_w0, r.own_w1, r.own_wqkv, r.own_wproj)
     mine = {}
-
-    def part(i, flip):
-        name, first, count, _ = out_units[i]
-        start = pl.multiple_of(at[flip] * block[name] + first, 16)
-        return gathered[name].at[pl.ds(start, count), :]
-
-    def out_start(chosen):
-        for flip in ("x", "y", "s"):
-            for i in chosen:
-                name, first, count, _ = out_units[i]
+    side = z % 2
+    z_peer = (me, z + 1 - 2 * side)
+
+    def part(i, flip, first, count):
+        third = own[i].shape[0] // 3
+        at_third = {-1: side, 0: 2 * side, 1: 1, 2: 2 - 2 * side, 3: 0}[first]
+        start = pl.multiple_of((at[flip] * 3 + at_third) * third, 16)
+        return gathered[i].at[pl.ds(start, count * third), :]
+
+    def own_part(i, first):
+        third = own[i].shape[0] // 3
+        return own[i].at[pl.ds(pl.multiple_of((2 * side if first == 0 else 1) * third, 16), third), :]
+
+    def pass_on(i, step, flip, first, count, target):
+        place = lambda: part(i, flip, first, count)
+        net.push((-1 - i, step), lambda: (place(), place(), target))
+
+    def out_start(i):
+        for first in (0, 1):
+            for axis in "xy":
                 net.push(
-                    (i, flip),
-                    lambda i=i, flip=flip, src=own[name].at[first : first + count, :]: (src, part(i, ""), peer[flip]),
+                    (-1 - i, axis + str(first)),
+                    lambda first=first, axis=axis: (own_part(i, first), part(i, "", first, 1), peer[axis]),
                 )
-        for i in chosen:
-            name, first, count, _ = out_units[i]
-            mine[i] = fetch(own[name].at[first : first + count, :], part(i, ""))
-
-    def out_pass(chosen):
-        for direct in (True, False):
-            for i in chosen:
-                axis = out_units[i][3]
-                if not direct:
-                    axis = OTHER[axis]
-                net.take((i, axis), part(i, axis), peer[axis])
-                if direct:
-                    net.push((i, "d"), lambda i=i, axis=axis: (part(i, axis), part(i, axis), peer[OTHER[axis]]))
-                net.push((i, "s" + axis), lambda i=i, axis=axis: (part(i, axis), part(i, axis), peer["s"]))
-
-    def out_late(chosen):
-        for i in chosen:
-            net.take((i, "d"), part(i, "d"), peer[OTHER[out_units[i][3]]])
-            net.push((i, "sd"), lambda i=i: (part(i, "d"), part(i, "d"), peer["s"]))
-
-    def out_end(chosen):
-        for i in chosen:
-            mine[i].wait()
-            for name, flip in (("s", "s"), ("sx", "xs"), ("sy", "ys"), ("sd", "ds")):
-                net.take((i, name), part(i, flip), peer["s"])
-
-    grads = dict(w0=r.grad_w0, w1=r.grad_w1, wqkv=r.grad_wqkv, wproj=r.grad_wproj)
-    results = dict(w0=r.out_w0, w1=r.out_w1, wqkv=r.out_wqkv, wproj=r.out_wproj)
+        net.push((-1 - i, "s"), lambda: (own[i], part(i, "", 3, 3), peer["s"]))
+        mine[i] = fetch(own[i], part(i, "", 3, 3))
+
+    def took(i, step, flip, first, count, source):
+        net.take((-1 - i, step), part(i, flip, first, count), source)
+
+    def out_first(i):
+        took(i, "x0", "x", 0, 1, peer["x"])
+        pass_on(i, "d0", "x", 0, 1, peer["y"])
+        pass_on(i, "zx", "x", 0, 1, z_peer)
+        took(i, "y0", "y", 0, 1, peer["y"])
+        pass_on(i, "zy", "y", 0, 1, z_peer)
+
+    def out_second(i):
+        took(i, "y1", "y", 1, 1, peer["y"])
+        pass_on(i, "d1", "y", 1, 1, peer["x"])
+        pass_on(i, "sy", "y", -1, 2, peer["s"])
+        took(i, "x1", "x", 1, 1, peer["x"])
+        pass_on(i, "sx", "x", -1, 2, peer["s"])
+
+    def out_third(i):
+        took(i, "d0", "d", 0, 1, peer["y"])
+        pass_on(i, "zd", "d", 0, 1, z_peer)
+
+    def out_fourth(i):
+        took(i, "d1", "d", 1, 1, peer["x"])
+        pass_on(i, "sd", "d", -1, 2, peer["s"])
+        took(i, "zx", "x", 2, 1, z_peer)
+        pass_on(i, "ox", "x", 2, 1, peer["s"])
+        took(i, "zy", "y", 2, 1, z_peer)
+        pass_on(i, "oy", "y", 2, 1, peer["s"])
+
+    def out_fifth(i):
+        took(i, "zd", "d", 2, 1, z_peer)
+        pass_on(i, "od", "d", 2, 1, peer["s"])
+
+    def out_end(i):
+        mine[i].wait()
+        took(i, "s", "s", 3, 3, peer["s"])
+        for flip in "xyd":
+            took(i, "s" + flip, flip + "s", -1, 2, peer["s"])
+            took(i, "o" + flip, flip + "s", 2, 1, peer["s"])
+
+    grads = dict(w0=r.grad_w0, w1=r.grad_w1, both=r.grad_both)
+    results = dict(w0=r.out_w0, w1=r.out_w1, both=r.out_both)
     done = []
 
     def unit_ref(i):
         name, first, count, low, width, _ = in_units[i]
         return grads[name], (slice(first, first + count), slice(low, low + width))
 
-    def in_core(chosen):
-        for i in chosen:
-            ref, span = unit_ref(i)
-            net.push((i, "a"), lambda i=i, ref=ref, span=span: (ref.at[(1 - core, slice(None), slice(None)) + span], r.ra[i], peer["s"]))
+    def in_core(i):
+        ref, span = unit_ref(i)
+        net.push((i, "a"), lambda i=i, ref=ref, span=span: (ref.at[(1 - core, slice(None), slice(None)) + span], r.ra[i], peer["s"]))
 
     def away(i):
         axis = in_units[i][5]
@@ -724,81 +806,73 @@
     def add_to(ref, where, value):
         ref[where] = ref[where] + value
 
-    def in_first(chosen):
-        for i in chosen:
-            ref, span = unit_ref(i)
-            axis = in_units[i][5]
-            net.take((i, "a"), r.ra[i], peer["s"])
-            add_to(ref, (core, slice(None), slice(None)) + span, r.ra[i][...])
-            net.push((i, "b"), lambda i=i, ref=ref, span=span, axis=axis: (ref.at[(core,) + away(i) + span], r.rb[i], peer[axis]))
-
-    def in_second(chosen):
-        for i in chosen:
-            ref, span = unit_ref(i)
-            axis = in_units[i][5]
-            net.take((i, "b"), r.rb[i], peer[axis])
-            add_to(ref, (core,) + near(i) + span, r.rb[i][...])
-            net.push((i, "c"), lambda i=i, ref=ref, span=span, axis=axis: (ref.at[(core,) + cross(i) + span], r.rc[i], peer[OTHER[axis]]))
+    def in_first(i):
+        ref, span = unit_ref(i)
+        axis = in_units[i][5]
+        net.take((i, "a"), r.ra[i], peer["s"])
+        add_to(ref, (core, slice(None), slice(None)) + span, r.ra[i][...])
+        net.push((i, "b"), lambda i=i, ref=ref, span=span, axis=axis: (ref.at[(core,) + away(i) + span], r.rb[i], peer[axis]))
+
+    def in_second(i):
+        ref, span = unit_ref(i)
+        axis = in_units[i][5]
+        net.take((i, "b"), r.rb[i], peer[axis])
+        add_to(ref, (core,) + near(i) + span, r.rb[i][...])
+        net.push((i, "c"), lambda i=i, ref=ref, span=span, axis=axis: (ref.at[(core,) + cross(i) + span], r.rc[i], peer[OTHER[axis]]))
 
     def z_out_of(i):
-        if i == "za":
-            return r.own_affine, r.rza
-        if i == "zr":
-            return r.own_rows, r.rzr
+        if i >= len(in_units):
+            return ((r.own_affine, r.rza), (r.own_rows, r.rzr))[i - len(in_units)]
         ref, span = unit_ref(i)
         return ref.at[(core, py, px) + span], r.rz[i]
 
-    def in_third(chosen):
-        for i in chosen:
-            ref, span = unit_ref(i)
-            net.take((i, "c"), r.rc[i], peer[OTHER[in_units[i][5]]])
-            add_to(ref, (core, py, px) + span, r.rc[i][...])
-            z_first([i])
-
-    def z_first(chosen):
-        for i in chosen:
-            src, slots = z_out_of(i)
-
-            @pl.when(outer)
-            def _():
-                net.copy((i, "z0"), src, slots.at[0], z_in).start()
-
-    def z_second(chosen):
-        for i in chosen:
-            src, slots = z_out_of(i)
-
-            @pl.when(inner)
-            def _():
-                net.take((i, "z0"), slots.at[0], z_out)
-                src[...] = src[...] + slots[0]
-                net.copy((i, "z1"), src, slots.at[1], z_cross).start()
-
-    def z_third(chosen):
-        for i in chosen:
-            src, slots = z_out_of(i)
-
-            @pl.when(inner)
-            def _():
-                net.take((i, "z1"), slots.at[1], z_cross)
-                slots[0] = src[...] + slots[1]
-                net.copy((i, "z2"), slots.at[0], slots.at[0], z_out).start()
-
-    def z_end(chosen):
-        for i in chosen:
-            src, slots = z_out_of(i)
-
-            @pl.when(outer)
-            def _():
-                net.take((i, "z2"), slots.at[0], z_in)
-
-            if i == "za":
-                target = r.out_affine
-            elif i == "zr":
-                target = r.out_rows
-            else:
-                name, first, count, low, width, _ = in_units[i]
-                target = results[name].at[first : first + count, low : low + width]
-            done.append(fetch(slots.at[0], target))
+    def in_third(i):
+        if i >= len(in_units):
+            z_first(i)
+            return
+        ref, span = unit_ref(i)
+        net.take((i, "c"), r.rc[i], peer[OTHER[in_units[i][5]]])
+        add_to(ref, (core, py, px) + span, r.rc[i][...])
+        z_first(i)
+
+    def z_first(i):
+        src, slots = z_out_of(i)
+
+        @pl.when(outer)
+        def _():
+            net.copy((i, "z0"), src, slots.at[0], z_in).start()
+
+    def z_second(i):
+        src, slots = z_out_of(i)
+
+        @pl.when(inner)
+        def _():
+            net.take((i, "z0"), slots.at[0], z_out)
+            src[...] = src[...] + slots[0]
+            net.copy((i, "z1"), src, slots.at[1], z_cross).start()
+
+    def z_third(i):
+        src, slots = z_out_of(i)
+
+        @pl.when(inner)
+        def _():
+            net.take((i, "z1"), slots.at[1], z_cross)
+            slots[0] = src[...] + slots[1]
+            net.copy((i, "z2"), slots.at[0], slots.at[0], z_out).start()
+
+    def z_end(i):
+        src, slots = z_out_of(i)
+
+        @pl.when(outer)
+        def _():
+            net.take((i, "z2"), slots.at[0], z_in)
+
+        if i >= len(in_units):
+            target = (r.out_affine, r.out_rows)[i - len(in_units)]
+        else:
+            name, first, count, low, width, _ = in_units[i]
+            target = results[name].at[first : first + count, low : low + width]
+        done.append(fetch(slots.at[0], target))
 
     def z_drain(chosen):
         for i in chosen:
@@ -812,6 +886,12 @@
             def _():
                 net.copy((i, "z1"), src, slots.at[1], z_cross).wait_send()
                 net.copy((i, "z2"), slots.at[0], slots.at[0], z_out).wait_send()
+
+    STEPS = (in_core, in_first, in_second, in_third, z_second, z_third, z_end)
+
+    def run(chosen):
+        for i, step in chosen:
+            STEPS[step](i)
 
     def keep(ref, rows_per):
         def store(row, col, value):
@@ -827,17 +907,13 @@
 
         return store
 
-    P0, P1 = [0, 1, 2], [3, 4, 5, 6]
-    P2, Q1, Q2 = [7, 8], [9, 10, 11, 12], [13, 14]
-    W0, W1, REST = [0, 1], [2, 3], [4, 5, 6]
-    copied_out = []
-    r.grad = r.out
+    r.grad = r.a2
     r.columns = column_spans(ch)
     r.live = lambda i: r.loads[0, i] > 0
     r.grad0, r.grad1 = keep(r.grad_w0, block["w0"]), keep(r.grad_w1, block["w1"])
-    keep_qkv, keep_proj = keep(r.grad_wqkv, block["wqkv"]), keep(r.grad_wproj, block["wproj"])
-    r.grad_qkv = lambda value: keep_qkv(0, 0, value)
-    r.grad_proj = lambda value: keep_proj(0, 0, value)
+    keep_both = keep(r.grad_both, block["wqkv"])
+    r.grad_qkv = lambda value: keep_both(0, 0, value)
+    r.grad_proj = lambda value: keep_both(0, 3 * ch, value)
 
     def exchange(what, src, slots):
         each = len(src.shape) == len(slots.shape)
@@ -873,90 +949,75 @@
             exchange("m", r.mod_out, r.mod_in)
             r.mod_in[pl.ds(me, 1)] = r.mod_out[pl.ds(me, 1)]
         if name == "w0":
-            out_pass(W0)
-            out_late(W0)
-            out_start(W1)
-            out_end(W0)
-        if name == "conv0":
-            out_pass(W1)
-            out_start(REST)
+            out_first(0)
+            out_second(0)
+            out_third(0)
+            out_start(1)
+            out_fourth(0)
+            out_fifth(0)
+            out_end(0)
+            out_first(1)
         if name == "affine":
             exchanged("m", r.mod_in)
             r.mod[...] = unpacked(jnp.sum(r.mod_in[...], axis=0), 2, wide_rows)
+            out_fourth(1)
         if name == "w1":
-            out_late(W1)
-            out_end(W1)
+            for i in (2, 3):
+                out_first(i)
+                out_second(i)
+            out_fifth(1)
+            out_end(1)
         if name == "wqkv":
-            out_pass(REST)
-            out_late(REST)
-            out_end(REST)
+            for i in (2, 3):
+                out_end(i)
             for copy in got_g:
                 copy.wait()
             for seg in segs:
                 rows = slice(seg.row, seg.row + seg.pixels)
                 r.g[rows, :] = jnp.where(r.live(seg.index), r.g[rows, :], 0).astype(BF)
-        if name == "out":
-            for seg, out in zip(segs, (r.big_out, r.small_out)):
-                copied_out.append(fetch(r.out.at[seg.row : seg.row + seg.pixels, :], out))
-        if name == "grad_qkv":
-            in_core(P0)
-        if name == "dr":
-            in_first(P0)
-        if name == ("grad1", 0):
-            in_core(P1)
-        if name == ("grad1", 1):
-            in_core(P2)
-            in_second(P0)
-            in_first(P1)
-        if name == "back1":
-            in_second(P1[:2])
-            z_second(P0)
-        if name == "dy0":
-            in_second(P1[2:])
+        if name == ("grad0", 0):
             exchanged("n", r.dmod_in)
             terms = unpacked_rows(r.dmod_in)
             grad = mm(r.embeds[...], terms, 0, 0)
             r.own_affine[...] = grad[0 : block["waff"], :].astype(BF)
-            z_first(["za"])
-            z_third(P0)
-        if name == ("grad0", 0):
-            in_core(Q1)
-            in_second(P2)
-            in_third(P1)
-        if name == ("grad0", 1):
-            in_core(Q2)
-            in_third(P2)
-            in_first(Q1)
-            z_end(P0)
-        if name == "back0":
-            in_second(Q1[2:])
-            in_second(Q2)
-            z_third(P2 + ["za"])
         if name == "rows":
             exchange("q", r.rows, r.rows_in)
             r.rows_in[pl.ds(me, 1)] = r.rows[...][None]
-        if name == "grad":
-            for copy in copied_out:
-                copy.wait()
+        if name == "late":
+            for seg, out in zip(segs, (r.big_out, r.small_out)):
+                done.append(fetch(r.out.at[seg.row : seg.row + seg.pixels, :], out))
+            exchanged("q", r.rows_in)
+            sums = jnp.concatenate(three_parts(jnp.sum(r.rows_in[...], axis=0)), axis=0).astype(BF)
+            lane = lax.broadcasted_iota(jnp.int32, (ch, 128), 1)
+            sub = lax.broadcasted_iota(jnp.int32, (ch, 128), 0)
+            per = ch // 8
+            cut = mm(sums, jnp.where((sub - per * me == lane) & (lane < per), 1.0, 0.0).astype(BF))
+            r.own_rows[...] = cut[0:16] + cut[16:32] + cut[32:48]
+        run(SCHEDULE.get(name, ()))
 
     def unpacked_rows(ref):
         values = ref[...].astype(F32)
         return jnp.concatenate([unpacked(values[o], 2, wide_rows) for o in range(8)], axis=0).astype(BF)
 
     def ticks(name):
-        if name == "back1":
+        if name == "conv0":
             return {
-                (0, 1): lambda: in_first(P2),
-                (0, 2): lambda: in_third(P0),
+                (0, 1): lambda: out_second(1),
+                (1, 0): lambda: (out_third(1), out_start(2), out_start(3)),
             }
-        if name == "back0":
+        if name == "conv1":
             return {
-                (0, 1): lambda: in_first(Q2),
-                (0, 2): lambda: z_second(P1),
-                (0, 3): lambda: in_second(Q1[:2]),
-                (1, 0): lambda: (z_second(P2 + ["za"]), z_third(P1)),
+                (0, 1): lambda: (out_third(2), out_third(3)),
+                (0, 2): lambda: (out_fourth(2), out_fourth(3)),
+                (1, 0): lambda: (out_fifth(2), out_fifth(3)),
             }
-        return {}
+        at_rows = type(name) is str
+        due = {
+            (key[1:] if at_rows else key[2]): chosen
+            for key, chosen in SCHEDULE.items()
+            if type(key) is tuple and len(key) == 3 and (key[0] == name if at_rows else key[:2] == name)
+        }
+        return {where: lambda chosen=chosen: run(chosen) for where, chosen in due.items()}
 
     def grad_affine(rows):
         r.dmod[...] = packed(jnp.concatenate(rows, axis=0), 16).astype(BF)
@@ -966,7 +1027,7 @@
     r.grad_affine = grad_affine
     exchange("p", r.message, r.messages)
     copied_message = fetch(r.message, r.messages.at[me])
-    out_start(W0)
+    out_start(0)
     r.waff[...] = jnp.zeros_like(r.waff)
     copied_affine = fetch(r.own_waff, r.waff.at[0 : block["waff"], :])
     got_g = [fetch(src, r.g.at[s.row : s.row + s.pixels, :]) for src, s in zip((r.big_g, r.small_g), segs)]
@@ -976,25 +1037,8 @@
 
     for seg, out in zip(segs, (r.big_grad, r.small_grad)):
         done.append(fetch(r.grad.at[seg.row : seg.row + seg.pixels, :], out))
-    exchanged("q", r.rows_in)
-    sums = jnp.concatenate(three_parts(jnp.sum(r.rows_in[...], axis=0)), axis=0).astype(BF)
-    lane = lax.broadcasted_iota(jnp.int32, (ch, 128), 1)
-    sub = lax.broadcasted_iota(jnp.int32, (ch, 128), 0)
-    per = ch // 8
-    cut = mm(sums, jnp.where((sub - per * me == lane) & (lane < per), 1.0, 0.0).astype(BF))
-    r.own_rows[...] = cut[0:16] + cut[16:32] + cut[32:48]
-    z_first(["zr"])
-    in_third(Q1[:2])
-    z_end(P1 + P2 + ["za"])
-    in_third(Q1[2:])
-    z_second(["zr"] + Q1[:2])
-    in_third(Q2)
-    z_second(Q1[2:])
-    z_third(["zr"] + Q1[:2])
-    z_second(Q2)
-    z_third(Q1[2:] + Q2)
-    z_end(["zr"] + Q1 + Q2)
-    z_drain(P0 + P1 + P2 + Q1 + Q2 + ["za", "zr"])
+    run(TAIL)
+    z_drain(range(len(in_units) + 2))
     net.drain()
     for copy in done:
         copy.wait()
@@ -1018,20 +1062,18 @@
         wproj=arrays["own_wproj"].shape[0],
     )
     segs, rows, _ = make_segs(sides)
-    out_units, in_units = gather_units(block), reduce_units(block, ch)
+    in_units = reduce_units(block, ch)
     width = dict(w0=ch, w1=ch, wqkv=3 * ch, wproj=ch)
     buffer = lambda *shape: pltpu.VMEM(shape, BF)
     wide_buffer = lambda *shape: pltpu.VMEM(shape, F32)
     whole = {name: buffer(8 * block[name], width[name]) for name in WEIGHTS}
-    grads = {name: buffer(2, 2, 2, block[name], width[name]) for name in WEIGHTS}
-    copies = len(transfer_names(out_units, in_units))
+    copies = len(transfer_names(in_units))
     scratch = dict(
         block_scratch(sides, ch),
         **whole,
-        grad_w0=grads["w0"],
-        grad_w1=grads["w1"],
-        grad_wqkv=grads["wqkv"],
-        grad_wproj=grads["wproj"],
+        grad_w0=buffer(2, 2, 2, block["w0"], ch),
+        grad_w1=buffer(2, 2, 2, block["w1"], ch),
+        grad_both=buffer(2, 2, 2, block["wqkv"], 4 * ch),
         x=buffer(rows, ch),
         g=buffer(rows, ch),
         out=buffer(rows, ch),
@@ -1070,8 +1112,7 @@
         out_affine=((block["waff"], 2 * ch), BF),
         out_w0=((block["w0"], ch), BF),
         out_w1=((block["w1"], ch), BF),
-        out_wqkv=((block["wqkv"], 3 * ch), BF),
-        out_wproj=((block["wproj"], ch), BF),
+        out_both=((block["wqkv"], 4 * ch), BF),
     )
     names = list(arrays) + list(outs) + list(scratch)
 
@@ -1096,10 +1137,12 @@
 
 
 def finish_call(results, per):
-    images, rows, weights = results[:4], results[4], results[5:]
+    images, both = results[:4], results[8]
+    ch = both.shape[1] // 4
     outs = [jax.ShapeDtypeStruct(image.shape, image.dtype) for image in images]
-    outs += [jax.ShapeDtypeStruct((3, per), F32), jax.ShapeDtypeStruct((10, per), F32)]
-    outs += [jax.ShapeDtypeStruct(weight.shape, F32) for weight in weights]
+    shapes = [(3, per), (10, per)] + [weight.shape for weight in results[5:8]]
+    shapes += [(both.shape[0], 3 * ch), (both.shape[0], ch)]
+    outs += [jax.ShapeDtypeStruct(shape, F32) for shape in shapes]
     total_in, total_out = len(results), len(outs)
 
     def kernel(*refs):
@@ -1116,10 +1159,16 @@
             copy.start()
             outward.append(copy)
 
-        for i in range(5, total_in):
+        for i in (8, 5, 6, 7):
             inward[i].wait()
-            made[i - 3][...] = held[i][...].astype(F32)
-            send(made[i - 3], targets[i + 1])
+            if i < 8:
+                made[i - 3][...] = held[i][...].astype(F32)
+                send(made[i - 3], targets[i + 1])
+            else:
+                made[5][...] = held[i][:, 0 : 3 * ch].astype(F32)
+                made[6][...] = held[i][:, 3 * ch :].astype(F32)
+                send(made[5], targets[9])
+                send(made[6], targets[10])
         for i in range(4):
             inward[i].wait()
             send(held[i], targets[i])

time: 155 us -> 138 us (0.89)
  Pallas kernels: 149 us -> 132 us
    pallas_call x1, Pallas kernels: 145 us -> 128 us  [fused_call(): pl.pallas_call(kernel, out_shape=[jax.ShapeDtypeStruct(*shape) for shape...]
where the time goes in v2:
time: 138 us; the launch traced here: 137 us
  Pallas kernels  132 us (96%)
  between operations  3.46 us (3%)
  other arithmetic  2.13 us (2%)
    pallas_call x1, Pallas kernels, fused_call(): pl.pallas_call(kernel, out_shape=[jax.ShapeDtypeStruct(*shape) for shape...  128 us
    pallas_call x1, Pallas kernels, finish_call(): pl.pallas_call(kernel, out_shape=outs, in_specs=[any_spec] * total_in, ou...  3.85 us

profile of v2, /device:TPU:0, one launch (start us, length us, event | category | flops | bytes accessed | tf_op | source)
XLA Modules:
  0.0 137.3 jit_solution(15426409525411121089)
XLA Ops:
  3.2 0.7 fusion.7
  4.0 0.8 fusion.11
  4.8 0.1 reshape.141
  4.9 0.6 fusion.1.refs_5_
  5.5 127.7 %shard_map.257 = (bf16[1024,384]{1,0:T(8,128)(2,1)}, bf16[256,384]{1,0:T(8,128)(2,1)}, bf16[1024,384]{1,0:T(8,128)(2,1)}, bf16[256,384]{1,0:T(8,128)(2,1)}, f32[...) custom-call(s32[1,2]{1,0:T(1,128)} %refs_0_.1, ...), custom_call_target="tpu_custom_call" | custom-call | tf_op jit(solution)/shard_map/pallas_call | solution.py:1126
  133.2 3.9 %shard_map.258 = (bf16[1024,384]{1,0:T(8,128)(2,1)}, bf16[256,384]{1,0:T(8,128)(2,1)}, bf16[1024,384]{1,0:T(8,128)(2,1)}, bf16[256,384]{1,0:T(8,128)(2,1)}, f32[...) custom-call(bf16[1024,384]{1,0:T(8,128)(2,1)} %get-tuple-element.31., ...), custom_call_target="tpu_custom_call" | custom-call | tf_op jit(solution)/shard_map/pallas_call | solution.py:1184
  (1 shorter events, 0.0 us)

commit v3 on v2

--- a/solution.py
+++ b/solution.py
@@ -267,28 +267,32 @@
             self.datt_t[pl.ds(self.row, self.head), self.at] = (self.dq * (1.0 / math.sqrt(self.head))).astype(BF)
 
 
-def attention(seg, block, chunk, keyvalue, qkv_t, datt_t, dkv):
+def attention(segs, keyvalue, qkv_t, datt_t, dkv):
     pair = 2 * datt_t.shape[0] // HEADS
-    span = slice(seg.row, seg.row + seg.pixels)
-    dkv[span, :] = jnp.zeros((seg.pixels, dkv.shape[1]), F32)
+    dkv[...] = jnp.zeros(dkv.shape, F32)
 
     def heads(index, carry):
         row = pl.multiple_of(index * pair, pair)
-        parts = [
-            HeadPart((qkv_t, datt_t, keyvalue, dkv), span, chunk, row, half, slice(first, first + block))
-            for first in range(span.start, span.stop, block)
-            for half in range(2)
-        ]
+        parts = []
+        for seg in segs:
+            span = slice(seg.row, seg.row + seg.pixels)
+            block, chunk = min(512, seg.pixels), min(256, seg.pixels)
+            for first in range(span.start, span.stop, block):
+                for half in range(2):
+                    at = slice(first, first + block)
+                    parts.append(HeadPart((qkv_t, datt_t, keyvalue, dkv), span, chunk, row, half, at))
+
+        def step(k, what, n):
+            if 0 <= k < len(parts) and n < parts[k].pixels // parts[k].chunk:
+                getattr(parts[k], what)(n)
+
+        chunks = max(part.pixels // part.chunk for part in parts)
         for k in range(-1, len(parts) + 2):
-            for n in range(seg.pixels // chunk):
-                if 0 <= k - 2 < len(parts):
-                    parts[k - 2].last_products(n)
-                if 0 <= k - 1 < len(parts):
-                    parts[k - 1].back(n)
-                if 0 <= k < len(parts):
-                    parts[k].attend(n)
-                if 0 <= k + 1 < len(parts):
-                    parts[k + 1].score(n)
+            for n in range(chunks):
+                step(k - 2, "last_products", n)
+                step(k - 1, "back", n)
+                step(k, "attend", n)
+                step(k + 1, "score", n)
         return carry
 
     lax.fori_loop(0, HEADS // 2, heads, 0)
@@ -354,7 +358,7 @@
             store_triple(triple, seg, start, a1, False)
             kept1[rows_at(seg.pad + start), :] = a1.astype(BF)
             return carry
-        each_block(seg, go, 0)
+        each_block(seg, go, 0, ticks("a1"))
 
     hook("w1")
     sums = []
@@ -393,8 +397,7 @@
         each_block(seg, go, 0)
 
     dkv = r.dkv
-    for seg in segs:
-        attention(seg, min(512, seg.pixels), min(256, seg.pixels), kv, qkv_t, datt_t, dkv)
+    attention(segs, kv, qkv_t, datt_t, dkv)
 
     hook("att")
     dqkv = r.dqkv
@@ -565,30 +568,32 @@
 
 SCHEDULE = {
     "grad_qkv": ((0, 0), (1, 0)),
-    ("dr", 0, 2): ((0, 1),),
-    ("dr", 0, 3): ((1, 1),),
-    "grad1": ((0, 2), (1, 2), (2, 0), (3, 0), (4, 0), (5, 0)),
-    ("back1", 0, 1): ((2, 1), (3, 1), (0, 3), (1, 3)),
-    ("back1", 0, 3): ((4, 1), (0, 4), (5, 1)),
-    "back1": ((1, 4), (0, 5), (2, 2), (3, 2)),
-    ("dy0", 1, 0): ((1, 5), (4, 2), (5, 2)),
-    ("grad0", 0, 1): ((2, 3), (3, 3)),
-    ("grad0", 0): ((4, 3), (5, 3), (12, 3), (6, 0), (7, 0), (2, 4), (8, 0), (9, 0)),
-    ("grad0", 1, 1): ((6, 1), (7, 1)),
-    ("grad0", 1, 2): ((3, 4),),
-    ("grad0", 1): ((10, 0), (11, 0), (8, 1), (2, 5), (9, 1)),
-    ("back0", 0, 1): ((4, 4), (3, 5), (6, 2), (7, 2)),
-    ("back0", 0, 2): ((5, 4), (10, 1), (11, 1)),
-    ("back0", 0, 3): ((4, 5), (8, 2), (7, 3), (6, 3), (9, 2), (12, 4)),
-    ("back0", 1, 0): ((5, 5),),
-    "back0": ((7, 4), (10, 2), (11, 2), (6, 4), (9, 3), (8, 3)),
-    ("late", 0, 1): ((12, 5),),
-    ("late", 0, 2): ((10, 3), (7, 5), (9, 4), (11, 3)),
-    ("late", 1, 0): ((6, 5), (8, 4)),
-    ("grad", 0, 0): ((9, 5), (10, 4), (13, 3)),
-    ("grad", 0, 2): ((11, 4), (13, 4), (8, 5)),
+    ("grad1", 0, 1): ((0, 1), (1, 1)),
+    "grad1": ((2, 0), (3, 0), (4, 0), (5, 0)),
+    ("back1", 0, 2): ((0, 2), (1, 2)),
+    ("back1", 0, 3): ((2, 1), (3, 1)),
+    ("dy0", 0, 0): ((0, 3), (1, 3), (0, 4), (5, 1), (4, 1)),
+    ("grad0", 0, 1): ((2, 2), (3, 2)),
+    ("grad0", 0): ((0, 5), (6, 0), (7, 0), (8, 0), (9, 0)),
+    ("grad0", 1, 1): ((4, 2), (5, 2)),
+    ("grad0", 1): ((10, 0), (11, 0)),
+    ("back0", 0, 0): ((6, 1),),
+    ("back0", 0, 1): ((2, 3), (1, 4), (3, 3), (2, 4), (7, 1)),
+    ("back0", 0, 2): ((4, 3), (3, 4), (5, 3), (4, 4), (8, 1), (9, 1)),
+    ("back0", 0, 3): ((0, 6),),
+    ("back0", 1, 0): ((6, 2), (10, 1), (1, 5)),
+    "back0": ((7, 2), (11, 1)),
+    ("late", 0, 0): ((2, 5), (8, 2)),
+    ("late", 0, 2): ((9, 2),),
+    ("late", 0, 3): ((3, 5),),
+    ("late", 1, 0): ((1, 6), (6, 3), (5, 4)),
+    ("grad", 0, 0): ((10, 2),),
+    ("grad", 0, 1): ((4, 5),),
+    ("grad", 0, 2): ((7, 3), (6, 4)),
+    ("grad", 0, 3): ((2, 6),),
+    ("grad", 1, 0): ((11, 2),),
 }
-TAIL = ((0, 6), (1, 6), (10, 5), (7, 6), (2, 6), (3, 6), (4, 6), (6, 6), (5, 6), (12, 6), (11, 5), (13, 5), (9, 6), (8, 6), (10, 6), (11, 6), (13, 6))
+TAIL = ((3, 6), (5, 5), (11, 4), (9, 3), (8, 4), (8, 3), (7, 4), (1, 7), (0, 7), (6, 5), (10, 3), (4, 6), (9, 4), (11, 5), (11, 3), (10, 4), (2, 7), (5, 6), (8, 5), (6, 6), (11, 6), (7, 5), (3, 7), (9, 5), (8, 6), (4, 7), (10, 5), (7, 6), (5, 7), (9, 6), (6, 7), (11, 7), (10, 6), (8, 7), (7, 7), (9, 7), (10, 7))
 
 
 class Net:
@@ -646,8 +651,8 @@
 def transfer_names(in_units):
     names = [(-1 - i, t) for i in range(len(WEIGHTS)) for t in OUT_STEPS]
     names += [(i, t) for i in range(len(in_units)) for t in "abc"]
-    names += [(i, t) for i in range(len(in_units) + 2) for t in ("z0", "z1", "z2")]
-    return names + [(what, flip) for what in SMALL for flip in FLIPS]
+    names += [(i, t) for i in range(len(in_units)) for t in ("z0", "z1", "z2")]
+    return names + [("n", 0), ("n", 1)] + [(what, flip) for what in SMALL for flip in FLIPS]
 
 
 def packed(rows, height):
@@ -683,6 +688,8 @@
     at = {flip: index(flip) for flip in FLIPS + ("",)}
     peer = {flip: (at[flip], z) for flip in FLIPS}
     z_in, z_out, z_cross = (me, jnp.where(z < 2, 1, 2)), (me, jnp.where(z < 2, 0, 3)), (me, 3 - z)
+    side = z % 2
+    z_peer = (me, z + 1 - 2 * side)
     net = Net(transfer_names(in_units), r.send, r.recv)
 
     local = []
@@ -699,22 +706,12 @@
     for flip in FLIPS:
         pl.semaphore_signal(barrier, inc=1, device_id=peer[flip], device_id_type=MESH)
 
-    @pl.when(outer)
-    def _():
-        pl.semaphore_signal(barrier, inc=1, device_id=z_in, device_id_type=MESH)
-
-    @pl.when(inner)
-    def _():
-        pl.semaphore_signal(barrier, inc=1, device_id=z_out, device_id_type=MESH)
-        pl.semaphore_signal(barrier, inc=1, device_id=z_cross, device_id_type=MESH)
-
-    pl.semaphore_wait(barrier, jnp.where(outer, 8, 9))
+    for target in (z_peer, z_cross):
+        pl.semaphore_signal(barrier, inc=1, device_id=target, device_id_type=MESH)
 
     gathered = [getattr(r, name) for name in WEIGHTS]
     own = (r.own_w0, r.own_w1, r.own_wqkv, r.own_wproj)
     mine = {}
-    side = z % 2
-    z_peer = (me, z + 1 - 2 * side)
 
     def part(i, flip, first, count):
         third = own[i].shape[0] // 3
@@ -738,7 +735,6 @@
                     lambda first=first, axis=axis: (own_part(i, first), part(i, "", first, 1), peer[axis]),
                 )
         net.push((-1 - i, "s"), lambda: (own[i], part(i, "", 3, 3), peer["s"]))
-        mine[i] = fetch(own[i], part(i, "", 3, 3))
 
     def took(i, step, flip, first, count, source):
         net.take((-1 - i, step), part(i, flip, first, count), source)
@@ -773,6 +769,19 @@
         took(i, "zd", "d", 2, 1, z_peer)
         pass_on(i, "od", "d", 2, 1, peer["s"])
 
+    def whole_start(i):
+        for flip, step in (("x", "x0"), ("y", "y0"), ("d", "d0"), ("s", "s")):
+            net.push((-1 - i, step), lambda flip=flip: (own[i], part(i, "", 3, 3), peer[flip]))
+
+    def whole_pass(i, flip):
+        took(i, flip + "0", flip, 3, 3, peer[flip])
+        pass_on(i, "s" + flip, flip, 3, 3, peer["s"])
+
+    def whole_end(i):
+        mine[i].wait()
+        for step, flip in (("s", "s"), ("sx", "xs"), ("sy", "ys"), ("sd", "ds")):
+            took(i, step, flip, 3, 3, peer["s"])
+
     def out_end(i):
         mine[i].wait()
         took(i, "s", "s", 3, 3, peer["s"])
@@ -820,22 +829,24 @@
         add_to(ref, (core,) + near(i) + span, r.rb[i][...])
         net.push((i, "c"), lambda i=i, ref=ref, span=span, axis=axis: (ref.at[(core,) + cross(i) + span], r.rc[i], peer[OTHER[axis]]))
 
+    z_units = [(r.grad_both, r.out_both, (slice(None), slice(None)))]
+    z_units += [unit_ref(i)[:1] + (results[in_units[i][0]],) + unit_ref(i)[1:] for i in range(2, len(in_units))]
+
     def z_out_of(i):
-        if i >= len(in_units):
-            return ((r.own_affine, r.rza), (r.own_rows, r.rzr))[i - len(in_units)]
-        ref, span = unit_ref(i)
+        if i >= len(z_units):
+            return r.own_rows, r.rzr
+        ref, _, span = z_units[i]
         return ref.at[(core, py, px) + span], r.rz[i]
 
     def in_third(i):
-        if i >= len(in_units):
-            z_first(i)
-            return
         ref, span = unit_ref(i)
         net.take((i, "c"), r.rc[i], peer[OTHER[in_units[i][5]]])
         add_to(ref, (core, py, px) + span, r.rc[i][...])
-        z_first(i)
 
     def z_first(i):
+        if i == len(z_units):
+            exchanged("q", r.rows_in)
+            r.own_rows[...] = jnp.sum(r.rows_in[...], axis=0)
         src, slots = z_out_of(i)
 
         @pl.when(outer)
@@ -867,11 +878,10 @@
         def _():
             net.take((i, "z2"), slots.at[0], z_in)
 
-        if i >= len(in_units):
-            target = (r.out_affine, r.out_rows)[i - len(in_units)]
+        if i >= len(z_units):
+            target = r.out_rows
         else:
-            name, first, count, low, width, _ = in_units[i]
-            target = results[name].at[first : first + count, low : low + width]
+            target = z_units[i][1].at[z_units[i][2]]
         done.append(fetch(slots.at[0], target))
 
     def z_drain(chosen):
@@ -887,7 +897,7 @@
                 net.copy((i, "z1"), src, slots.at[1], z_cross).wait_send()
                 net.copy((i, "z2"), slots.at[0], slots.at[0], z_out).wait_send()
 
-    STEPS = (in_core, in_first, in_second, in_third, z_second, z_third, z_end)
+    STEPS = (in_core, in_first, in_second, in_third, z_first, z_second, z_third, z_end)
 
     def run(chosen):
         for i, step in chosen:
@@ -951,65 +961,71 @@
         if name == "w0":
             out_first(0)
             out_second(0)
+            out_start(1)
             out_third(0)
-            out_start(1)
             out_fourth(0)
             out_fifth(0)
+            out_first(1)
             out_end(0)
-            out_first(1)
         if name == "affine":
             exchanged("m", r.mod_in)
             r.mod[...] = unpacked(jnp.sum(r.mod_in[...], axis=0), 2, wide_rows)
-            out_fourth(1)
         if name == "w1":
-            for i in (2, 3):
-                out_first(i)
-                out_second(i)
             out_fifth(1)
             out_end(1)
         if name == "wqkv":
-            for i in (2, 3):
-                out_end(i)
+            net.drain()
+            whole_end(2)
+            whole_end(3)
             for copy in got_g:
                 copy.wait()
             for seg in segs:
                 rows = slice(seg.row, seg.row + seg.pixels)
                 r.g[rows, :] = jnp.where(r.live(seg.index), r.g[rows, :], 0).astype(BF)
         if name == ("grad0", 0):
-            exchanged("n", r.dmod_in)
-            terms = unpacked_rows(r.dmod_in)
-            grad = mm(r.embeds[...], terms, 0, 0)
-            r.own_affine[...] = grad[0 : block["waff"], :].astype(BF)
+            exchanged("n", r.planes.at[z, 0:8])
+            net.push(("n", 0), lambda: (r.planes.at[z], r.planes.at[z], z_peer))
+        if name == ("grad0", 1):
+            pair = z - side
+            net.take(("n", 0), r.planes.at[z + 1 - 2 * side], z_peer)
+            net.push(("n", 1), lambda: (r.planes.at[pl.ds(pair, 2)], r.planes.at[pl.ds(pair, 2)], z_cross))
+        if name == "back0":
+            net.take(("n", 1), r.planes.at[pl.ds(2 - (z - side), 2)], z_cross)
+            values = r.planes[...].astype(F32)
+            terms = [unpacked(values[p, o], 2, wide_rows) for p in range(4) for o in range(8)]
+            embeds = [values[p, 8] for p in range(4)]
+            grad = mm(jnp.concatenate(embeds, axis=0).astype(BF), jnp.concatenate(terms, axis=0).astype(BF), 0, 0)
+            r.own_affine[...] = grad[0 : block["waff"], :]
+            done.append(fetch(r.own_affine, r.out_affine))
         if name == "rows":
-            exchange("q", r.rows, r.rows_in)
-            r.rows_in[pl.ds(me, 1)] = r.rows[...][None]
+            per = ch // 8
+            lane = lax.broadcasted_iota(jnp.int32, (ch, 8 * 128), 1)
+            sub = lax.broadcasted_iota(jnp.int32, (ch, 8 * 128), 0)
+            spread = jnp.where((sub // per == lane // 128) & (sub % per == lane % 128), 1.0, 0.0).astype(BF)
+            cut = mm(jnp.concatenate(three_parts(r.rows[...]), axis=0).astype(BF), spread)
+            cut = cut[0:16] + cut[16:32] + cut[32:48]
+            for o in range(8):
+                r.rows_out[o] = cut[:, 128 * o : 128 * (o + 1)]
+            exchange("q", r.rows_out, r.rows_in)
+            r.rows_in[pl.ds(me, 1)] = r.rows_out[pl.ds(me, 1)]
         if name == "late":
             for seg, out in zip(segs, (r.big_out, r.small_out)):
                 done.append(fetch(r.out.at[seg.row : seg.row + seg.pixels, :], out))
-            exchanged("q", r.rows_in)
-            sums = jnp.concatenate(three_parts(jnp.sum(r.rows_in[...], axis=0)), axis=0).astype(BF)
-            lane = lax.broadcasted_iota(jnp.int32, (ch, 128), 1)
-            sub = lax.broadcasted_iota(jnp.int32, (ch, 128), 0)
-            per = ch // 8
-            cut = mm(sums, jnp.where((sub - per * me == lane) & (lane < per), 1.0, 0.0).astype(BF))
-            r.own_rows[...] = cut[0:16] + cut[16:32] + cut[32:48]
         run(SCHEDULE.get(name, ()))
-
-    def unpacked_rows(ref):
-        values = ref[...].astype(F32)
-        return jnp.concatenate([unpacked(values[o], 2, wide_rows) for o in range(8)], axis=0).astype(BF)
 
     def ticks(name):
         if name == "conv0":
             return {
                 (0, 1): lambda: out_second(1),
-                (1, 0): lambda: (out_third(1), out_start(2), out_start(3)),
+                (0, 2): lambda: (whole_start(2), whole_start(3)),
+                (1, 0): lambda: out_third(1),
             }
+        if name == "a1":
+            return {(0, 3): lambda: out_fourth(1)}
         if name == "conv1":
             return {
-                (0, 1): lambda: (out_third(2), out_third(3)),
-                (0, 2): lambda: (out_fourth(2), out_fourth(3)),
-                (1, 0): lambda: (out_fifth(2), out_fifth(3)),
+                (0, 1): lambda: [whole_pass(i, flip) for i in (2, 3) for flip in "xy"],
+                (0, 3): lambda: [whole_pass(i, "d") for i in (2, 3)],
             }
         at_rows = type(name) is str
         due = {
@@ -1021,25 +1037,31 @@
 
     def grad_affine(rows):
         r.dmod[...] = packed(jnp.concatenate(rows, axis=0), 16).astype(BF)
-        exchange("n", r.dmod, r.dmod_in)
-        r.dmod_in[pl.ds(me, 1)] = r.dmod[...][None]
+        exchange("n", r.dmod, r.planes.at[z, 0:8])
+        r.planes[z, me] = r.dmod[...]
+        r.planes[z, 8] = r.embeds[...]
 
     r.grad_affine = grad_affine
+    pl.semaphore_wait(barrier, len(FLIPS) + 2)
     exchange("p", r.message, r.messages)
-    copied_message = fetch(r.message, r.messages.at[me])
     out_start(0)
     r.waff[...] = jnp.zeros_like(r.waff)
     copied_affine = fetch(r.own_waff, r.waff.at[0 : block["waff"], :])
+    copied_message = fetch(r.message, r.messages.at[me])
     got_g = [fetch(src, r.g.at[s.row : s.row + s.pixels, :]) for src, s in zip((r.big_g, r.small_g), segs)]
+    for i in range(len(WEIGHTS)):
+        mine[i] = fetch(own[i], part(i, "", 3, 3))
     for copy in got_x:
         copy.wait()
     block_body(sides, r, hook, ticks)
 
     for seg, out in zip(segs, (r.big_grad, r.small_grad)):
         done.append(fetch(r.grad.at[seg.row : seg.row + seg.pixels, :], out))
-    run(TAIL)
-    z_drain(range(len(in_units) + 2))
+    run(TAIL[:-8])
     net.drain()
+    z_drain(range(5))
+    run(TAIL[-8:])
+    z_drain(range(5, len(z_units) + 1))
     for copy in done:
         copy.wait()
 
@@ -1085,11 +1107,11 @@
         mod_in=wide_buffer(8, 16, 128),
         mod=wide_buffer(2, 2 * ch),
         dmod=buffer(16, 128),
-        dmod_in=buffer(8, 16, 128),
-        own_affine=buffer(block["waff"], 2 * ch),
-        rza=buffer(2, block["waff"], 2 * ch),
+        planes=buffer(4, 9, 16, 128),
+        own_affine=wide_buffer(block["waff"], 2 * ch),
         rows=wide_buffer(16, ch),
-        rows_in=wide_buffer(8, 16, ch),
+        rows_out=wide_buffer(8, 16, 128),
+        rows_in=wide_buffer(8, 16, 128),
         own_rows=wide_buffer(16, 128),
         rzr=wide_buffer(2, 16, 128),
         send=pltpu.SemaphoreType.DMA((copies,)),
@@ -1100,7 +1122,7 @@
         [buffer(2, 2, n, w) for _, _, n, _, w, _ in in_units],
         [buffer(2, n, w) for _, _, n, _, w, _ in in_units],
         [buffer(n, w) for _, _, n, _, w, _ in in_units],
-        [buffer(2, n, w) for _, _, n, _, w, _ in in_units],
+        [buffer(2, block["wqkv"], 4 * ch)] + [buffer(2, n, w) for _, _, n, _, w, _ in in_units[2:]],
     ]
     big, small = segs[0].pixels, segs[1].pixels
     outs = dict(
@@ -1109,7 +1131,7 @@
         big_grad=((big, ch), BF),
         small_grad=((small, ch), BF),
         out_rows=((16, 128), F32),
-        out_affine=((block["waff"], 2 * ch), BF),
+        out_affine=((block["waff"], 2 * ch), F32),
         out_w0=((block["w0"], ch), BF),
         out_w1=((block["w1"], ch), BF),
         out_both=((block["wqkv"], 4 * ch), BF),
@@ -1161,7 +1183,9 @@
 
         for i in (8, 5, 6, 7):
             inward[i].wait()
-            if i < 8:
+            if i == 5:
+                send(held[i], targets[i + 1])
+            elif i < 8:
                 made[i - 3][...] = held[i][...].astype(F32)
                 send(made[i - 3], targets[i + 1])
             else:

time: 138 us -> 135 us (0.978)
  Pallas kernels: 132 us -> 129 us
    pallas_call x1, Pallas kernels: 128 us -> 125 us  [fused_call(): pl.pallas_call(kernel, out_shape=[jax.ShapeDtypeStruct(*shape) for shape...]
where the time goes in v3:
time: 135 us
  Pallas kernels  129 us (96%)
  between operations  3.46 us (3%)
  other arithmetic  2.13 us (2%)
    pallas_call x1, Pallas kernels, fused_call(): pl.pallas_call(kernel, out_shape=[jax.ShapeDtypeStruct(*shape) for shape...  125 us
    pallas_call x1, Pallas kernels, finish_call(): pl.pallas_call(kernel, out_shape=outs, in_specs=[any_spec] * total_in, ou...  3.9 us

profile of v3, /device:TPU:0, one launch (start us, length us, event | category | flops | bytes accessed | tf_op | source)
XLA Modules:
  0.0 134.7 jit_solution(7022684156500085240)
XLA Ops:
  3.2 0.7 fusion.7
  4.0 0.8 fusion.11
  4.8 0.1 reshape.141
  4.9 0.6 fusion.1.refs_5_
  5.5 125.1 %shard_map.257 = (bf16[1024,384]{1,0:T(8,128)(2,1)}, bf16[256,384]{1,0:T(8,128)(2,1)}, bf16[1024,384]{1,0:T(8,128)(2,1)}, bf16[256,384]{1,0:T(8,128)(2,1)}, f32[...) custom-call(s32[1,2]{1,0:T(1,128)} %refs_0_.1, ...), custom_call_target="tpu_custom_call" | custom-call | tf_op jit(solution)/shard_map/pallas_call | solution.py:1148
  130.6 3.9 %shard_map.258 = (bf16[1024,384]{1,0:T(8,128)(2,1)}, bf16[256,384]{1,0:T(8,128)(2,1)}, bf16[1024,384]{1,0:T(8,128)(2,1)}, bf16[256,384]{1,0:T(8,128)(2,1)}, f32[...) custom-call(bf16[1024,384]{1,0:T(8,128)(2,1)} %get-tuple-element.31., ...), custom_call_target="tpu_custom_call" | custom-call | tf_op jit(solution)/shard_map/pallas_call | solution.py:1208
  (1 shorter events, 0.0 us)
